TPU v7x, 512 devices: a whole 4x8x8 slice. The times are simulated.
512 devices in a mesh: gx: 64 (over z, y_hi, x), gy: 8 (over y_lo, core).
Axes of the slice: x: 4, y: 8 (y_hi: 2, y_lo: 4; y = y_hi * 4 + y_lo), z: 8, core: 2. Of those that a mesh axis runs over, the one named last changes fastest.
Arguments:
- features: bfloat16 [3584, 32, 5120], P('gx', None, 'gy'), may hold values from -6 to 6
- weight_x: int32 [3584], P('gx'), may hold values from 1 to 16
- weight_y: int32 [320], P('gy'), may hold values from 1 to 16
- conv_weight: bfloat16 [32, 32], replicated, may hold values from -1 to 1
- class_bias: float32 [32], replicated, may hold values from -4 to 4
Outputs:
- level0: bfloat16 [3072, 32, 4096], P('gx', None, 'gy')
- level1: bfloat16 [1536, 32, 1024], P('gx', None, 'gy')
- level2: bfloat16 [768, 32, 256], P('gx', None, 'gy')
- level3: bfloat16 [384, 32, 64], P('gx')
- level4: bfloat16 [192, 32, 16], P('gx')
All inputs are finite; a program needn't handle non-finite values.
Results may differ from a plain program's by a relative error of at most 0.006.
Values may be sent and summed in bfloat16 or wider, within the bound.
A program may use at most 64 MiB of HBM per device.

v0:
```python
import jax
import jax.numpy as jnp
from jax import lax
from jax.sharding import PartitionSpec as P

MARGIN = 8


def shifted(value, axis, steps):
    count = lax.axis_size(axis)
    initial, last = (max(0, -steps), min(count, count - steps))
    return lax.ppermute(value, axis, [(source, source + steps) for source in range(initial, last)])


def pooling(rows_y, depth):
    source = jnp.arange(rows_y * depth, dtype=jnp.int32)
    target = source // depth // 2 * (depth // 2) + source % depth // 2
    columns = jnp.arange(rows_y // 2 * (depth // 2), dtype=jnp.int32)
    return jnp.where(target[:, None] == columns[None, :], 0.125, 0.0).astype(jnp.float32)


def shrink(volume, rows_y, depth):
    xs, ks, width = volume.shape
    paired = volume.reshape(xs // 2, 2, ks, width).astype(jnp.float32)
    summed = paired[:, 0] + paired[:, 1]
    table = pooling(rows_y, depth)
    pooled = jnp.einsum(
        "xkv,vw->xkw",
        summed,
        table,
        precision=lax.Precision.HIGHEST,
        preferred_element_type=jnp.float32,
    )
    return pooled.astype(jnp.bfloat16)


def shards(features, weight_x, weight_y, conv_weight, class_bias):
    xe = features.shape[0]
    ye = weight_y.shape[0]
    depth = features.shape[2] // ye
    core_x = xe - MARGIN
    core_y = ye - MARGIN
    cut = core_y * depth
    logits = jnp.einsum("xcv,ck->xkv", features, conv_weight, preferred_element_type=jnp.float32)
    logits = (logits + class_bias[None, :, None]).astype(jnp.bfloat16)
    wx = weight_x.astype(jnp.float32)
    wy = weight_y.astype(jnp.float32)
    wyz = jnp.repeat(wy, depth)
    numer = logits.astype(jnp.float32) * (wx[:, None, None] * wyz[None, None, :])
    denom = wx[:, None] * wy[None, :]
    recv_n, recv_d = shifted((numer[core_x:], denom[core_x:]), "gx", 1)
    numer = numer[:core_x].at[:MARGIN].add(recv_n)
    denom = denom[:core_x].at[:MARGIN].add(recv_d)
    side_n, side_d = (
        shifted(numer[:, :, cut:].astype(jnp.bfloat16), "gy", 1).astype(jnp.float32),
        shifted(denom[:, core_y:].astype(jnp.bfloat16), "gy", 1).astype(jnp.float32),
    )
    numer = numer[:, :, :cut].at[:, :, : MARGIN * depth].add(side_n)
    denom = denom[:, :core_y].at[:, :MARGIN].add(side_d)
    denom_z = jnp.repeat(denom, depth, axis=1)
    blended = (numer / denom_z[:, None, :]).astype(jnp.bfloat16)
    first = shrink(blended, core_y, depth)
    second = shrink(first, core_y // 2, depth // 2)
    third = shrink(second, core_y // 4, depth // 4)
    whole_third = lax.all_gather(third, "gy", axis=2, tiled=True)
    fourth = shrink(whole_third, core_y // 8 * lax.axis_size("gy"), depth // 8)
    return (blended, first, second, whole_third, fourth)


def solution(mesh):
    placed = (P("gx", None, "gy"), P("gx"), P("gy"), P(), P())
    return jax.shard_map(
        shards,
        mesh=mesh,
        in_specs=placed,
        out_specs=(
            P("gx", None, "gy"),
            P("gx", None, "gy"),
            P("gx", None, "gy"),
            P("gx", None, None),
            P("gx", None, None),
        ),
        check_vma=False,
    )
```

profile of v0, /device:TPU:265, one launch (start us, length us, event | category | flops | bytes accessed | tf_op | source)
XLA Modules:
  0.0 79.2 jit_solution(5073156674485008796)
XLA Ops:
  0.6 0.8 %convert_element_type.64 = f32[40]{0:T(128)S(1)} convert(s32[40]{0:T(128)} %param.15) | non-fusion elementwise | flops 40 | bytes 320 | tf_op jit(solution)/shard_map/convert_element_type | solution.py:47
  1.5 0.1 broadcast_in_dim.50
  1.5 0.1 mul.73
  1.6 0.7 convert_element_type.63
  2.3 0.1 broadcast_multiply_fusion
  2.4 1.5 %multiply_bitcast_fusion = f32[56,32,640]{2,1,0:T(8,128)S(1)} fusion(f32[56,640]{1,0:T(8,128)S(1)} %broadcast_multiply_fusion, f32[32]{0:T(128)} %param.17, bf16[56,32,640]{2,1,0:T(8,128)(2,1)S(1)} %copy-done, bf16[32,32]{1,0:T(8,128)(2,1)} %param.16), kind=kOutput, calls=%fused_computation | convolution fusion | flops 77987840 | bytes 7026816 | tf_op jit(solution)/shard_map/xcv,ck->xkv/dot_general | solution.py:44
  3.9 3.1 %collective-permute-start = (f32[8,32,640]{2,1,0:T(8,128)S(1)}, f32[8,32,640]{2,1,0:T(8,128)S(1)}, u32[]{:S(2)}, u32[]{:S(2)}) collective-permute-start(f32[8,32,640]{2,1,0:T(8,128)S(1)} %slice.162), channel_id=1, source_target_pairs={{0,8},{8,16},{16,24},{24,32},{32,40},{40,48},{48,56},{56,64},{64,7... | collective-permute-start | bytes 1966088 | tf_op jit(solution)/shard_map/ppermute | solution.py:12
  7.1 0.1 broadcast_multiply_fusion.1
  7.1 0.1 slice.168
  7.2 3.1 %collective-permute-start.2 = (f32[8,40]{0,1:T(8,128)S(1)}, f32[8,40]{0,1:T(8,128)S(1)}, u32[]{:S(2)}, u32[]{:S(2)}) collective-permute-start(f32[8,40]{0,1:T(8,128)S(1)} %slice.168), channel_id=1, source_target_pairs={{0,8},{8,16},{16,24},{24,32},{32,40},{40,48},{48,56},{56,64},{64,7... | collective-permute-start | bytes 3848 | tf_op jit(solution)/shard_map/ppermute | solution.py:12
  10.3 0.3 slice.160
  10.6 33.1 %collective-permute-done = f32[8,32,640]{2,1,0:T(8,128)S(1)} collective-permute-done((f32[8,32,640]{2,1,0:T(8,128)S(1)}, f32[8,32,640]{2,1,0:T(8,128)S(1)}, u32[]{:S(2)}, u32[]{:S(2)}) %collective-permute-start) | collective-permute-done | bytes 655392 | tf_op jit(solution)/shard_map/ppermute | solution.py:12
  43.9 1.9 %copy-done.1 = f32[48,32,640]{2,1,0:T(8,128)} copy-done((f32[48,32,640]{2,1,0:T(8,128)}, f32[48,32,640]{2,1,0:T(8,128)S(1)}, u32[]{:S(2)}) %copy-start.1) | copy-done | bytes 3932184
  45.8 4.9 %collective-permute-start.1 = (bf16[48,32,128]{2,1,0:T(8,128)(2,1)S(1)}, bf16[48,32,128]{2,1,0:T(8,128)(2,1)S(1)}, u32[]{:S(2)}, u32[]{:S(2)}) collective-permute-start(bf16[48,32,128]{2,1,0:T(8,128)(2,1)S(1)} %slice.224), channel_id=1, source_target_pairs={{0,1},{1,2},{2,3},{3,4},{4,5},{5,6},{6,7},{8,9},{9,10},{10,11},{11... | collective-permute-start | bytes 1179656 | tf_op jit(solution)/shard_map/ppermute | solution.py:12
  50.7 0.3 scatter-add.16
  51.0 1.9 %collective-permute-start.3 = (bf16[48,8]{0,1:T(8,128)(2,1)S(1)}, bf16[48,8]{0,1:T(8,128)(2,1)S(1)}, u32[]{:S(2)}, u32[]{:S(2)}) collective-permute-start(bf16[48,8]{0,1:T(8,128)(2,1)S(1)} %slice.225), channel_id=1, source_target_pairs={{0,1},{1,2},{2,3},{3,4},{4,5},{5,6},{6,7},{8,9},{9,10},{10,11},{11... | collective-permute-start | bytes 2312 | tf_op jit(solution)/shard_map/ppermute | solution.py:12
  52.9 0.6 compare_reduce_fusion
  53.6 1.8 %collective-permute-done.3 = bf16[48,8]{0,1:T(8,128)(2,1)S(1)} collective-permute-done((bf16[48,8]{0,1:T(8,128)(2,1)S(1)}, bf16[48,8]{0,1:T(8,128)(2,1)S(1)}, u32[]{:S(2)}, u32[]{:S(2)}) %collective-permute-start.3) | collective-permute-done | bytes 800 | tf_op jit(solution)/shard_map/ppermute | solution.py:12
  55.4 0.6 fusion.30
  56.1 0.1 copy.21
  56.2 2.2 %slice.163 = f32[48,32,512]{2,1,0:T(8,128)S(1)} slice(f32[48,32,640]{2,1,0:T(8,128)} %copy-done.1), slice={[0:48], [0:32], [0:512]} | slice | bytes 6291456 | tf_op jit(solution)/shard_map/slice | solution.py:58
  58.4 1.3 %fusion.7 = f32[48,32,512]{2,1,0:T(8,128)S(1)} fusion(f32[48,32,512]{2,1,0:T(8,128)S(1)} %slice.163, f32[48,32,640]{2,1,0:T(8,128)} %copy-done.1, bf16[48,32,128]{2,1,0:T(8,128)(2,1)S(1)} %collective-permute-done.1), kind=kLoop, calls=%fused_computation.14 | loop fusion | flops 393216 | bytes 1966080 | tf_op jit(solution)/shard_map/scatter-add | solution.py:58
  59.7 0.5 divide_convert_fusion
  60.3 0.4 convert.12
  60.7 1.5 %fusion.4 = bf16[24,32,128]{2,1,0:T(8,128)(2,1)S(1)} fusion(f32[24,2,32,512]{3,2,1,0:T(8,128)S(1)} %convert.12, s32[512]{0:T(512)S(1)} %fusion.42), kind=kOutput, calls=%fused_computation.8 | convolution fusion | flops 604602368 | bytes 3344384 | tf_op jit(solution)/shard_map/xkv,vw->xkw/dot_general | solution.py:27
  62.2 0.3 convolution_convert_fusion
  62.6 0.5 convolution_convert_fusion.2
  63.1 14.3 %all_gather.3 = bf16[6,32,64]{1,2,0:T(8,128)(2,1)S(1)} all-gather(bf16[6,32,8]{1,2,0:T(8,128)(2,1)S(1)} %convolution_convert_fusion.2), channel_id=1, replica_groups=mesh['gx'=64,'gy'=8] {'gy'}, dimensions={2}, use_global_device_ids=true | all-gather | bytes 27648 | tf_op jit(solution)/shard_map/all_gather | solution.py:65
  77.4 0.7 copy.30
  78.1 0.1 copy.39
  78.2 0.1 copy.40
  78.3 0.9 %convolution_convert_fusion.1 = bf16[3,32,16]{1,2,0:T(8,128)(2,1)} fusion(f32[3,1,32,64]{3,2,0,1:T(8,128)S(1)} %copy.39, f32[3,1,32,64]{3,2,0,1:T(8,128)S(1)} %copy.40, s32[64]{0:T(128)S(1)} %fusion.55), kind=kOutput, calls=%fused_computation.10 | convolution fusion | flops 1189376 | bytes 52480 | tf_op jit(solution)/shard_map/xkv,vw->xkw/dot_general | solution.py:27
  (25 shorter events, 0.3 us)
Async XLA Ops:
  0.6 1.7 %copy-start = (bf16[56,32,640]{2,1,0:T(8,128)(2,1)S(1)}, bf16[56,32,640]{2,1,0:T(8,128)(2,1)}, u32[]{:S(2)}) copy-start(bf16[56,32,640]{2,1,0:T(8,128)(2,1)} %param.13) | copy-start | bytes 6881284
  3.9 39.8 %collective-permute-start = (f32[8,32,640]{2,1,0:T(8,128)S(1)}, f32[8,32,640]{2,1,0:T(8,128)S(1)}, u32[]{:S(2)}, u32[]{:S(2)}) collective-permute-start(f32[8,32,640]{2,1,0:T(8,128)S(1)} %slice.162), channel_id=1, source_target_pairs={{0,8},{8,16},{16,24},{24,32},{32,40},{40,48},{48,56},{56,64},{64,7... | collective-permute-start | bytes 1966088 | tf_op jit(solution)/shard_map/ppermute | solution.py:12
  7.2 43.5 %collective-permute-start.2 = (f32[8,40]{0,1:T(8,128)S(1)}, f32[8,40]{0,1:T(8,128)S(1)}, u32[]{:S(2)}, u32[]{:S(2)}) collective-permute-start(f32[8,40]{0,1:T(8,128)S(1)} %slice.168), channel_id=1, source_target_pairs={{0,8},{8,16},{16,24},{24,32},{32,40},{40,48},{48,56},{56,64},{64,7... | collective-permute-start | bytes 3848 | tf_op jit(solution)/shard_map/ppermute | solution.py:12
  43.8 1.9 %copy-start.1 = (f32[48,32,640]{2,1,0:T(8,128)}, f32[48,32,640]{2,1,0:T(8,128)S(1)}, u32[]{:S(2)}) copy-start(f32[48,32,640]{2,1,0:T(8,128)S(1)} %fusion.8) | copy-start | bytes 11796484
  45.8 12.7 %collective-permute-start.1 = (bf16[48,32,128]{2,1,0:T(8,128)(2,1)S(1)}, bf16[48,32,128]{2,1,0:T(8,128)(2,1)S(1)}, u32[]{:S(2)}, u32[]{:S(2)}) collective-permute-start(bf16[48,32,128]{2,1,0:T(8,128)(2,1)S(1)} %slice.224), channel_id=1, source_target_pairs={{0,1},{1,2},{2,3},{3,4},{4,5},{5,6},{6,7},{8,9},{9,10},{10,11},{11... | collective-permute-start | bytes 1179656 | tf_op jit(solution)/shard_map/ppermute | solution.py:12
  51.0 4.4 %collective-permute-start.3 = (bf16[48,8]{0,1:T(8,128)(2,1)S(1)}, bf16[48,8]{0,1:T(8,128)(2,1)S(1)}, u32[]{:S(2)}, u32[]{:S(2)}) collective-permute-start(bf16[48,8]{0,1:T(8,128)(2,1)S(1)} %slice.225), channel_id=1, source_target_pairs={{0,1},{1,2},{2,3},{3,4},{4,5},{5,6},{6,7},{8,9},{9,10},{10,11},{11... | collective-permute-start | bytes 2312 | tf_op jit(solution)/shard_map/ppermute | solution.py:12
  60.3 1.9 %copy-start.2 = (bf16[48,32,512]{2,1,0:T(8,128)(2,1)}, bf16[48,32,512]{2,1,0:T(8,128)(2,1)S(1)}, u32[]{:S(2)}) copy-start(bf16[48,32,512]{2,1,0:T(8,128)(2,1)S(1)} %divide_convert_fusion) | copy-start | bytes 4718596
  62.2 17.0 %copy-start.3 = (bf16[24,32,128]{2,1,0:T(8,128)(2,1)}, bf16[24,32,128]{2,1,0:T(8,128)(2,1)S(1)}, u32[]{:S(2)}) copy-start(bf16[24,32,128]{2,1,0:T(8,128)(2,1)S(1)} %fusion.4) | copy-start | bytes 589828
  62.6 16.6 %copy-start.4 = (bf16[12,32,32]{2,1,0:T(8,128)(2,1)}, bf16[12,32,32]{2,1,0:T(8,128)(2,1)S(1)}, u32[]{:S(2)}) copy-start(bf16[12,32,32]{2,1,0:T(8,128)(2,1)S(1)} %convolution_convert_fusion) | copy-start | bytes 73732
where the time goes:
time: 79.5 us; the launch traced here: 79.2 us
  waiting for transfers between devices  35 us (44%)
  blocking collectives  14.3 us (18%)
  starting transfers between devices  13 us (16%)
  local copies, waits for them, and re-layouts  6.01 us (8%)
  other arithmetic  5.29 us (7%)
  matrix products  4.66 us (6%)
  between operations  0.93 us (1%)
    ppermute x4, waiting for transfers between devices, shifted(): lax.ppermute(value, axis, [(source, source + steps) for source in range(i...  35 us
    all_gather x1, blocking collectives, shards(): whole_third = lax.all_gather(third, 'gy', axis=2, tiled=True)  14.3 us
    ppermute x4, starting transfers between devices, shifted(): lax.ppermute(value, axis, [(source, source + steps) for source in range(i...  13 us
    dot_general x4, matrix products, shrink(): jnp.einsum('xkv,vw->xkw', summed, table, precision=lax.Precision.HIGHEST,...  3.15 us
    unnamed x13, local copies, waits for them, and re-layouts  2.77 us
    slice x1, local copies, waits for them, and re-layouts, shards(): numer = numer[:, :, :cut].at[:, :, :MARGIN * depth].add(side_n)  2.23 us
  transfers between devices with their start and end apart: 4, of which 2 were waited for; matrix products, arithmetic and copies ran while one was open for 6% of the time, Pallas kernels for 0%

commit v1 on v0

v1 whole, which is shorter than its diff:
```python
import jax
import jax.numpy as jnp
from jax import lax
from jax.experimental import pallas as pl
from jax.experimental.pallas import tpu as pltpu
from jax.sharding import PartitionSpec as P

MESH = pl.DeviceIdType.MESH
F32 = jnp.float32
BF16 = jnp.bfloat16

CHUNKS = 6
ROWS = 256
PIECES = ((1, 0), (1, 1), (2, 0), (2, 1), (3, 0), (3, 1), (0, 0), (0, 1))
WAYS = (2, -2, 2, -2, -2, -2, 2, -2, 2)


def iota(shape, dim):
    return lax.broadcasted_iota(jnp.int32, shape, dim)


def one_hot(condition, value):
    return jnp.where(condition, value, 0.0).astype(BF16)


def dot(a, b):
    return jnp.dot(a, b, preferred_element_type=F32)


def device(x, y, z, core):
    return (z * 8 + (y // 4) * 4 + x, (y % 4) * 2 + core)


def kernel(
    features,
    weight_x,
    weight_y,
    conv,
    bias,
    level0,
    level1,
    level2,
    level3,
    level4,
    held,
    block,
    out0,
    out1,
    y_out,
    y_in,
    corner_out,
    corner_in,
    x_out,
    x_in,
    xw_out,
    xw_in,
    relay,
    relay_w,
    first_y,
    shares,
    pool1,
    pool2,
    pool3,
    pool4,
    own_third,
    all_third,
    load_sem,
    store_sem,
    y_send,
    y_recv,
    x_send,
    x_recv,
    hop_send,
    hop_recv,
    on_send,
    third_send,
    third_recv,
):
    gx = lax.axis_index("gx")
    gy = lax.axis_index("gy")
    x, z, core = gx % 4, gx // 8, gy % 2
    y = (gx // 4) % 2 * 4 + gy // 2
    near = x < 3
    far = jnp.logical_and(x == 3, gx < 63)
    has_left = gx > 0
    has_up = gy > 0
    has_down = gy < 7

    def carries(way):
        source = (y - way + 8) % 8
        last = jnp.logical_and(z == 7, source >= 4)
        return jnp.logical_and(x == 0, jnp.logical_not(last))

    def carry_to(way):
        source = (y - way + 8) % 8
        return device(0, (source + 4) % 8, z + source // 4, core)

    far_in = jnp.logical_and(x == 0, has_left)

    loads = [
        pltpu.make_async_copy(features.at[i], held.at[i], load_sem.at[i])
        for i in range(7)
    ]
    loads[6].start()
    for i in range(CHUNKS):
        loads[i].start()

    barrier = pltpu.get_barrier_semaphore()

    def greet(target):
        pl.semaphore_signal(barrier, inc=1, device_id=target, device_id_type=MESH)

    for way in (2, -2):

        @pl.when(carries(way))
        def _():
            greet(device(3, (y - way + 8) % 8, z, core))

        @pl.when(far_in)
        def _():
            before = z - jnp.where(y < 4, 1, 0)
            greet(device(0, (y + 4 + way) % 8, before, core))

    @pl.when(jnp.logical_and(has_left, x > 0))
    def _():
        greet((gx - 1, gy))

    for o in range(1, 8):
        greet((gx, (gy + o) % 8))

    pick = (iota((ROWS, 32), 0) % 32) == iota((ROWS, 32), 1)
    spread = one_hot(pick, 1.0)
    dims = (((1,), (1,)), ((), ()))
    tall = lax.dot_general(spread, conv[...], dims, preferred_element_type=F32)
    wide = lax.dot_general(
        tall.astype(BF16), spread, dims, preferred_element_type=F32
    )
    same = iota((ROWS, ROWS), 0) // 32 == iota((ROWS, ROWS), 1) // 32
    block[...] = jnp.where(same, wide, 0.0).astype(BF16)
    bias_column = jnp.sum(jnp.where(pick, bias[...], 0.0), axis=1, keepdims=True)

    def logits(i):
        return (dot(block[...], held[i]) + bias_column).astype(BF16)

    lane_y = iota((8, 128), 1) // 16
    row = iota((8, 128), 0)
    wy_own = jnp.zeros((8, 128), F32)
    wy_last = jnp.zeros((8, 128), F32)
    wx_own = jnp.zeros((8, 128), F32)
    wx_last = jnp.zeros((8, 128), F32)
    for k in range(8):
        wy_own = jnp.where(lane_y == k, weight_y[k].astype(F32), wy_own)
        wy_last = jnp.where(lane_y == k, weight_y[32 + k].astype(F32), wy_last)
        wx_own = jnp.where(row == k, weight_x[k].astype(F32), wx_own)
        wx_last = jnp.where(row == k, weight_x[48 + k].astype(F32), wx_last)
    corner_out[ROWS:, :] = jnp.concatenate([wy_last, wy_last], axis=0).astype(BF16)
    xw_out[...] = jnp.concatenate([wx_last, wx_last], axis=0).astype(BF16)

    loads[6].wait()
    margin = logits(6)
    corner_out[:ROWS, :] = margin[:, 512:]
    for t in range(4):
        x_out[t] = margin[:, 128 * t : 128 * (t + 1)]

    peers = 7 + near.astype(jnp.int32) + 2 * far.astype(jnp.int32)
    for way in (2, -2):
        peers = peers + carries(way).astype(jnp.int32)
    pl.semaphore_wait(barrier, peers)

    def remote(src, dst, send, recv, target):
        return pltpu.make_async_remote_copy(
            src_ref=src,
            dst_ref=dst,
            send_sem=send,
            recv_sem=recv,
            device_id=target,
            device_id_type=MESH,
        )

    down = (gx, (gy + 1) % 8)
    corner_copy = remote(corner_out, corner_in, y_send.at[6], y_recv.at[6], down)
    y_copies = [
        remote(y_out.at[i], y_in.at[i], y_send.at[i], y_recv.at[i], down)
        for i in range(CHUNKS)
    ]

    def part(ref, h):
        t, half = PIECES[h]
        return ref.at[t, pl.ds(128 * half, 128)]

    def direct(h):
        target = ((gx + 1) % 64, gy)
        src, dst = (xw_out, xw_in) if h == 8 else (part(x_out, h), part(x_in, h))
        return remote(src, dst, x_send.at[h], x_recv.at[h], target)

    def hop(h):
        target = device(0, (y + WAYS[h] + 8) % 8, z, core)
        src, dst = (xw_out, relay_w) if h == 8 else (part(x_out, h), relay.at[h])
        return remote(src, dst, hop_send.at[h], hop_recv.at[h], target)

    def onward(h):
        target = carry_to(WAYS[h])
        src, dst = (relay_w, xw_in) if h == 8 else (relay.at[h], part(x_in, h))
        return remote(src, dst, on_send.at[h], x_recv.at[h], target)

    def send_x(pieces):
        @pl.when(near)
        def _():
            for h in pieces:
                direct(h).start()

        @pl.when(far)
        def _():
            for h in pieces:
                hop(h).start()

    @pl.when(has_down)
    def _():
        corner_copy.start()

    send_x((8, 0, 1, 2, 3, 4, 5))

    for i in range(CHUNKS):
        loads[i].wait()
        value = logits(i)
        y_out[i] = value[:, 512:]
        out0[i] = value[:, :512]

        @pl.when(has_down)
        def _():
            y_copies[i].start()

        if i == 3:
            @pl.when(has_up)
            def _():
                corner_copy.wait_recv()
                wy_up = corner_in[ROWS:, :].astype(F32)[:8]
                total = wy_own + wy_up
                own_share, up_share = wy_own / total, wy_up / total
                shares[0] = own_share
                shares[1] = up_share
                x_out[0] = (
                    x_out[0].astype(F32) * own_share[:1]
                    + corner_in[:ROWS, :].astype(F32) * up_share[:1]
                ).astype(BF16)

            send_x((6, 7))

    source, target = iota((512, 128), 0), iota((512, 128), 1)
    pool1[...] = one_hot(source // 32 * 8 + source % 16 // 2 == target, 0.125)
    source, target = iota((128, 128), 0), iota((128, 128), 1)
    pool2[...] = one_hot(source // 16 * 4 + source % 8 // 2 == target, 0.125)
    pool3[...] = one_hot(
        jnp.logical_and(
            source // 8 * 2 + source % 4 // 2 + gy * 8 == target, source < 32
        ),
        0.125,
    )
    pool4[...] = one_hot(jnp.logical_and(source // 4 == target, source < 64), 0.125)

    for h in (8, 0, 1, 2, 3, 4, 5, 6, 7):

        @pl.when(carries(WAYS[h]))
        def _():
            hop(h).wait_recv()
            onward(h).start()

    third = jnp.zeros((16, 128), F32)

    def mips(i, third):
        pooled = dot(out0[i], pool1[...]).reshape(4, 2, 32, 128)
        first = (pooled[:, 0] + pooled[:, 1]).astype(BF16).reshape(128, 128)
        out1[i] = first
        pltpu.make_async_copy(out0.at[i], level0.at[i], store_sem.at[i]).start()
        pltpu.make_async_copy(out1.at[i], level1.at[i], store_sem.at[6 + i]).start()
        pooled = dot(first, pool2[...]).reshape(2, 2, 32, 128)
        second = (pooled[:, 0] + pooled[:, 1]).astype(BF16).reshape(64, 128)
        level2[pl.ds(64 * i, 64), :] = second[:, :32]
        pooled = dot(second, pool3[...])
        pooled = pooled[:32] + pooled[32:]
        third = third + pltpu.roll(pooled[:16], 8 * i, 1)
        return third + pltpu.roll(pooled[16:], 8 * (6 + i), 1)

    for i in range(1, CHUNKS):

        @pl.when(has_up)
        def _():
            y_copies[i].wait_recv()
            out0[i, :, :128] = (
                out0[i, :, :128].astype(F32) * shares[0, :1]
                + y_in[i].astype(F32) * shares[1, :1]
            ).astype(BF16)

        third = mips(i, third)

    first_y[...] = out0[0, :, :128].astype(F32)

    @pl.when(has_up)
    def _():
        y_copies[0].wait_recv()
        first_y[...] = first_y[...] * shares[0, :1] + y_in[0].astype(F32) * shares[1, :1]

    out0[0, :, :128] = first_y[...].astype(BF16)

    @pl.when(has_left)
    def _():
        for h in (8, 0, 1, 2, 3, 4, 5, 6, 7):
            direct(h).wait_recv()
        wx_left = xw_in[...].astype(F32)[:8]
        total = wx_own + wx_left
        own_share, left_share = wx_own / total, wx_left / total
        for a in range(8):
            rows = pl.ds(32 * a, 32)
            mine, theirs = own_share[a : a + 1], left_share[a : a + 1]
            for t in range(4):
                lanes = pl.ds(128 * t, 128)
                own = first_y[rows, :] if t == 0 else out0[0, rows, lanes].astype(F32)
                out0[0, rows, lanes] = (
                    own * mine + x_in[t, rows, :].astype(F32) * theirs
                ).astype(BF16)

    third = mips(0, third)

    own_third[...] = third.astype(BF16)
    third_copies = [
        remote(
            own_third,
            all_third.at[o],
            third_send.at[o],
            third_recv.at[o],
            (gx, (gy + o) % 8),
        )
        for o in range(1, 8)
    ]
    for copy in third_copies:
        copy.start()
    for copy in third_copies:
        copy.wait_recv()
    group = iota((16, 128), 1) // 8
    parts = [own_third[...].astype(F32)] + [
        all_third[o].astype(F32) for o in range(1, 8)
    ]
    rows = [None] * 12
    for q in range(12):
        owner = (group - q + 16) % 16
        value = jnp.zeros((16, 128), F32)
        for o in range(8):
            value = jnp.where(owner == (gy - o + 8) % 8, parts[o], value)
        half, i = q // 6, q % 6
        rows[2 * i + half] = pltpu.roll(value, (128 - 8 * q) % 128, 1)
    whole = jnp.concatenate(rows, axis=0).astype(BF16)
    level3[...] = whole[:, :64]
    pooled = dot(whole, pool4[...]).reshape(3, 2, 32, 128)
    fourth = (pooled[:, 0] + pooled[:, 1]).astype(BF16).reshape(96, 128)
    level4[...] = fourth[:, :16]

    for copy in third_copies:
        copy.wait_send()

    @pl.when(has_down)
    def _():
        corner_copy.wait_send()
        for i in range(CHUNKS):
            y_copies[i].wait_send()

    @pl.when(near)
    def _():
        for h in range(9):
            direct(h).wait_send()

    @pl.when(far)
    def _():
        for h in range(9):
            hop(h).wait_send()

    for h in range(9):

        @pl.when(carries(WAYS[h]))
        def _():
            onward(h).wait_send()

    for i in range(CHUNKS):
        pltpu.make_async_copy(out0.at[i], level0.at[i], store_sem.at[i]).wait()
        pltpu.make_async_copy(out1.at[i], level1.at[i], store_sem.at[6 + i]).wait()


def shards(features, weight_x, weight_y, conv_weight, class_bias):
    vmem = pl.BlockSpec(memory_space=pltpu.VMEM)
    smem = pl.BlockSpec(memory_space=pltpu.SMEM)
    hbm = pl.BlockSpec(memory_space=pl.ANY)
    dma = pltpu.SemaphoreType.DMA
    outs = pl.pallas_call(
        kernel,
        name="blend",
        out_shape=(
            jax.ShapeDtypeStruct((6, 256, 512), BF16),
            jax.ShapeDtypeStruct((6, 128, 128), BF16),
            jax.ShapeDtypeStruct((384, 32), BF16),
            jax.ShapeDtypeStruct((192, 64), BF16),
            jax.ShapeDtypeStruct((96, 16), BF16),
        ),
        in_specs=[hbm, smem, smem, vmem, vmem],
        out_specs=(hbm, hbm, vmem, vmem, vmem),
        scratch_shapes=[
            pltpu.VMEM((7, 256, 640), BF16),
            pltpu.VMEM((256, 256), BF16),
            pltpu.VMEM((6, 256, 512), BF16),
            pltpu.VMEM((6, 128, 128), BF16),
            pltpu.VMEM((6, 256, 128), BF16),
            pltpu.VMEM((6, 256, 128), BF16),
            pltpu.VMEM((272, 128), BF16),
            pltpu.VMEM((272, 128), BF16),
            pltpu.VMEM((4, 256, 128), BF16),
            pltpu.VMEM((4, 256, 128), BF16),
            pltpu.VMEM((16, 128), BF16),
            pltpu.VMEM((16, 128), BF16),
            pltpu.VMEM((8, 128, 128), BF16),
            pltpu.VMEM((16, 128), BF16),
            pltpu.VMEM((256, 128), F32),
            pltpu.VMEM((2, 8, 128), F32),
            pltpu.VMEM((512, 128), BF16),
            pltpu.VMEM((128, 128), BF16),
            pltpu.VMEM((128, 128), BF16),
            pltpu.VMEM((128, 128), BF16),
            pltpu.VMEM((16, 128), BF16),
            pltpu.VMEM((8, 16, 128), BF16),
            dma((7,)),
            dma((12,)),
            dma((7,)),
            dma((7,)),
            dma((9,)),
            dma((9,)),
            dma((9,)),
            dma((9,)),
            dma((9,)),
            dma((8,)),
            dma((8,)),
        ],
        compiler_params=pltpu.CompilerParams(
            collective_id=0, has_side_effects=True, vmem_limit_bytes=24 << 20
        ),
    )(
        features.reshape(7, 256, 640),
        weight_x,
        weight_y,
        conv_weight,
        class_bias.reshape(1, 32),
    )
    return (
        outs[0].reshape(48, 32, 512),
        outs[1].reshape(24, 32, 128),
        outs[2].reshape(12, 32, 32),
        outs[3].reshape(6, 32, 64),
        outs[4].reshape(3, 32, 16),
    )


def solution(mesh):
    placed = (P("gx", None, "gy"), P("gx"), P("gy"), P(), P())
    return jax.shard_map(
        shards,
        mesh=mesh,
        in_specs=placed,
        out_specs=(
            P("gx", None, "gy"),
            P("gx", None, "gy"),
            P("gx", None, "gy"),
            P("gx", None, None),
            P("gx", None, None),
        ),
        check_vma=False,
    )
```

time: 79.5 us -> 39.4 us (0.50)
  the two profiles are of different devices: /device:TPU:265 before, /device:TPU:385 now
where the time goes in v1:
time: 39.4 us; the launch traced here: 39.2 us
  Pallas kernels  30.5 us (77%)
  local copies, waits for them, and re-layouts  8.06 us (20%)
  between operations  0.66 us (2%)
    pallas_call x1, Pallas kernels, shards(): pl.pallas_call(kernel, name='blend', out_shape=(jax.ShapeDtypeStruct((6,...  30.5 us
    unnamed x15, local copies, waits for them, and re-layouts  8.06 us

profile of v1, /device:TPU:385, one launch (start us, length us, event | category | flops | bytes accessed | tf_op | source)
XLA Modules:
  0.0 39.2 jit_solution(14068009997515786555)
XLA Ops:
  0.6 0.0 copy-start
  0.6 1.6 %copy-done = bf16[56,32,640]{2,1,0:T(8,128)(2,1)S(1)} copy-done((bf16[56,32,640]{2,1,0:T(8,128)(2,1)S(1)}, bf16[56,32,640]{2,1,0:T(8,128)(2,1)}, u32[]{:S(2)}) %copy-start) | copy-done | bytes 2293784
  2.3 0.0 copy-start.1
  2.3 0.7 %copy-done.1 = bf16[32,32]{1,0:T(8,128)(2,1)S(1)} copy-done((bf16[32,32]{1,0:T(8,128)(2,1)S(1)}, bf16[32,32]{1,0:T(8,128)(2,1)}, u32[]{:S(2)}) %copy-start.1) | copy-done | bytes 2072
  3.0 0.0 copy-start.2
  3.0 0.7 %copy-done.2 = s32[56]{0:T(128)S(1)} copy-done((s32[56]{0:T(128)S(1)}, s32[56]{0:T(128)}, u32[]{:S(2)}) %copy-start.2) | copy-done | bytes 248
  3.6 0.0 copy-start.3
  3.6 0.7 %copy-done.3 = s32[40]{0:T(128)S(1)} copy-done((s32[40]{0:T(128)S(1)}, s32[40]{0:T(128)}, u32[]{:S(2)}) %copy-start.3) | copy-done | bytes 184
  4.3 0.0 copy-start.4
  4.3 0.7 %copy-done.4 = f32[32]{0:T(128)S(1)} copy-done((f32[32]{0:T(128)S(1)}, f32[32]{0:T(128)}, u32[]{:S(2)}) %copy-start.4) | copy-done | bytes 152
  4.9 30.5 %blend.1 = (bf16[6,256,512]{2,1,0:T(8,128)(2,1)S(1)}, bf16[6,128,128]{2,1,0:T(8,128)(2,1)S(1)}, bf16[384,32]{1,0:T(8,128)(2,1)S(1)}, bf16[192,64]{1,0:T(8,128)(2,1)S(1)}, bf16[96,16]{1,0:T(8,128)(2,1)S(1)}) custom-call(bf16[7,256,640]{2,1,0:T(8,128)(2,1)S(1)} %bitcast.7, s32[56]{0:T(128)S(1)} %copy-done.2, s32[40]{0:T(128)S(1)} %copy-done.3, ...), custom_call_target="tpu_custom_call" | custom-call | tf_op jit(solution)/shard_map/blend/pallas_call | solution.py:392
  35.4 0.7 %copy.10 = bf16[3,32,16]{1,2,0:T(8,128)(2,1)} copy(bf16[3,32,16]{2,1,0:T(8,128)(2,1)S(1)} %bitcast.12) | data formatting | bytes 6144
  36.1 1.1 %copy.15 = bf16[48,32,512]{2,1,0:T(8,128)(2,1)} copy(bf16[48,32,512]{2,1,0:T(8,128)(2,1)S(1)} %bitcast.8) | data formatting | bytes 3145728
  37.2 0.7 %copy.16 = bf16[24,32,128]{2,1,0:T(8,128)(2,1)} copy(bf16[24,32,128]{2,1,0:T(8,128)(2,1)S(1)} %bitcast.9) | data formatting | bytes 393216
  37.9 0.6 %copy.17 = bf16[12,32,32]{2,1,0:T(8,128)(2,1)} copy(bf16[12,32,32]{2,1,0:T(8,128)(2,1)S(1)} %bitcast.10) | data formatting | bytes 49152
  38.5 0.6 %copy.18 = bf16[6,32,64]{2,1,0:T(8,128)(2,1)} copy(bf16[6,32,64]{2,1,0:T(8,128)(2,1)S(1)} %bitcast.11) | data formatting | bytes 49152
Async XLA Ops:
  0.6 1.6 %copy-start = (bf16[56,32,640]{2,1,0:T(8,128)(2,1)S(1)}, bf16[56,32,640]{2,1,0:T(8,128)(2,1)}, u32[]{:S(2)}) copy-start(bf16[56,32,640]{2,1,0:T(8,128)(2,1)} %param.5) | copy-start | bytes 6881284
  2.3 0.7 %copy-start.1 = (bf16[32,32]{1,0:T(8,128)(2,1)S(1)}, bf16[32,32]{1,0:T(8,128)(2,1)}, u32[]{:S(2)}) copy-start(bf16[32,32]{1,0:T(8,128)(2,1)} %conv.1) | copy-start | bytes 6148
  3.0 0.7 %copy-start.2 = (s32[56]{0:T(128)S(1)}, s32[56]{0:T(128)}, u32[]{:S(2)}) copy-start(s32[56]{0:T(128)} %weight_x.1) | copy-start | bytes 676
  3.6 0.7 %copy-start.3 = (s32[40]{0:T(128)S(1)}, s32[40]{0:T(128)}, u32[]{:S(2)}) copy-start(s32[40]{0:T(128)} %weight_y.1) | copy-start | bytes 484
  4.3 0.7 %copy-start.4 = (f32[32]{0:T(128)S(1)}, f32[32]{0:T(128)}, u32[]{:S(2)}) copy-start(f32[32]{0:T(128)} %param.9) | copy-start | bytes 388

commit v2 on v1

--- a/solution.py
+++ b/solution.py
@@ -33,19 +33,21 @@
 
 def kernel(
     features,
+    weight_x_in,
+    weight_y_in,
+    conv_in,
+    bias_in,
+    out0,
+    out1,
+    level2,
+    level3,
+    level4,
     weight_x,
     weight_y,
     conv,
     bias,
-    level0,
-    level1,
-    level2,
-    level3,
-    level4,
     held,
     block,
-    out0,
-    out1,
     y_out,
     y_in,
     corner_out,
@@ -65,7 +67,6 @@
     own_third,
     all_third,
     load_sem,
-    store_sem,
     y_send,
     y_recv,
     x_send,
@@ -101,8 +102,11 @@
         pltpu.make_async_copy(features.at[i], held.at[i], load_sem.at[i])
         for i in range(7)
     ]
-    loads[6].start()
-    for i in range(CHUNKS):
+    loads.append(pltpu.make_async_copy(conv_in, conv, load_sem.at[7]))
+    loads.append(pltpu.make_async_copy(bias_in, bias, load_sem.at[8]))
+    loads.append(pltpu.make_async_copy(weight_x_in, weight_x, load_sem.at[9]))
+    loads.append(pltpu.make_async_copy(weight_y_in, weight_y, load_sem.at[10]))
+    for i in (7, 8, 9, 10, 6, 0, 1, 2, 3, 4, 5):
         loads[i].start()
 
     barrier = pltpu.get_barrier_semaphore()
@@ -127,6 +131,9 @@
 
     for o in range(1, 8):
         greet((gx, (gy + o) % 8))
+
+    for i in (7, 8, 9, 10):
+        loads[i].wait()
 
     pick = (iota((ROWS, 32), 0) % 32) == iota((ROWS, 32), 1)
     spread = one_hot(pick, 1.0)
@@ -271,8 +278,6 @@
         pooled = dot(out0[i], pool1[...]).reshape(4, 2, 32, 128)
         first = (pooled[:, 0] + pooled[:, 1]).astype(BF16).reshape(128, 128)
         out1[i] = first
-        pltpu.make_async_copy(out0.at[i], level0.at[i], store_sem.at[i]).start()
-        pltpu.make_async_copy(out1.at[i], level1.at[i], store_sem.at[6 + i]).start()
         pooled = dot(first, pool2[...]).reshape(2, 2, 32, 128)
         second = (pooled[:, 0] + pooled[:, 1]).astype(BF16).reshape(64, 128)
         level2[pl.ds(64 * i, 64), :] = second[:, :32]
@@ -351,8 +356,9 @@
     whole = jnp.concatenate(rows, axis=0).astype(BF16)
     level3[...] = whole[:, :64]
     pooled = dot(whole, pool4[...]).reshape(3, 2, 32, 128)
-    fourth = (pooled[:, 0] + pooled[:, 1]).astype(BF16).reshape(96, 128)
-    level4[...] = fourth[:, :16]
+    fourth = pooled[:, 0] + pooled[:, 1]
+    for t in range(3):
+        level4[pl.ds(16 * t, 16), :] = fourth[t].T[:16].astype(BF16)
 
     for copy in third_copies:
         copy.wait_send()
@@ -379,33 +385,40 @@
         def _():
             onward(h).wait_send()
 
-    for i in range(CHUNKS):
-        pltpu.make_async_copy(out0.at[i], level0.at[i], store_sem.at[i]).wait()
-        pltpu.make_async_copy(out1.at[i], level1.at[i], store_sem.at[6 + i]).wait()
+
+def store(*refs):
+    sems = refs[10]
+    copies = [pltpu.make_async_copy(refs[i], refs[5 + i], sems.at[i]) for i in range(5)]
+    for copy in copies:
+        copy.start()
+    for copy in copies:
+        copy.wait()
 
 
 def shards(features, weight_x, weight_y, conv_weight, class_bias):
     vmem = pl.BlockSpec(memory_space=pltpu.VMEM)
-    smem = pl.BlockSpec(memory_space=pltpu.SMEM)
-    hbm = pl.BlockSpec(memory_space=pl.ANY)
+    hbm = pl.BlockSpec(memory_space=pltpu.HBM)
     dma = pltpu.SemaphoreType.DMA
+    shapes = (
+        jax.ShapeDtypeStruct((6, 256, 512), BF16),
+        jax.ShapeDtypeStruct((6, 128, 128), BF16),
+        jax.ShapeDtypeStruct((384, 32), BF16),
+        jax.ShapeDtypeStruct((192, 64), BF16),
+        jax.ShapeDtypeStruct((48, 32), BF16),
+    )
     outs = pl.pallas_call(
         kernel,
         name="blend",
-        out_shape=(
-            jax.ShapeDtypeStruct((6, 256, 512), BF16),
-            jax.ShapeDtypeStruct((6, 128, 128), BF16),
-            jax.ShapeDtypeStruct((384, 32), BF16),
-            jax.ShapeDtypeStruct((192, 64), BF16),
-            jax.ShapeDtypeStruct((96, 16), BF16),
-        ),
-        in_specs=[hbm, smem, smem, vmem, vmem],
-        out_specs=(hbm, hbm, vmem, vmem, vmem),
+        out_shape=shapes,
+        in_specs=[hbm] * 5,
+        out_specs=(vmem,) * 5,
         scratch_shapes=[
+            pltpu.SMEM((56,), jnp.int32),
+            pltpu.SMEM((40,), jnp.int32),
+            pltpu.VMEM((32, 32), BF16),
+            pltpu.VMEM((1, 32), F32),
             pltpu.VMEM((7, 256, 640), BF16),
             pltpu.VMEM((256, 256), BF16),
-            pltpu.VMEM((6, 256, 512), BF16),
-            pltpu.VMEM((6, 128, 128), BF16),
             pltpu.VMEM((6, 256, 128), BF16),
             pltpu.VMEM((6, 256, 128), BF16),
             pltpu.VMEM((272, 128), BF16),
@@ -424,8 +437,7 @@
             pltpu.VMEM((128, 128), BF16),
             pltpu.VMEM((16, 128), BF16),
             pltpu.VMEM((8, 16, 128), BF16),
-            dma((7,)),
-            dma((12,)),
+            dma((11,)),
             dma((7,)),
             dma((7,)),
             dma((9,)),
@@ -440,18 +452,32 @@
             collective_id=0, has_side_effects=True, vmem_limit_bytes=24 << 20
         ),
     )(
-        features.reshape(7, 256, 640),
-        weight_x,
-        weight_y,
-        conv_weight,
-        class_bias.reshape(1, 32),
-    )
+        *(
+            pltpu.with_memory_space_constraint(value, pltpu.HBM)
+            for value in (
+                features.reshape(7, 256, 640),
+                weight_x,
+                weight_y,
+                conv_weight,
+                class_bias.reshape(1, 32),
+            )
+        )
+    )
+    outs = pl.pallas_call(
+        store,
+        name="store",
+        out_shape=shapes,
+        in_specs=[pl.BlockSpec(memory_space=pl.ANY)] * 5,
+        out_specs=(hbm,) * 5,
+        scratch_shapes=[dma((5,))],
+        compiler_params=pltpu.CompilerParams(vmem_limit_bytes=1 << 20),
+    )(*outs)
     return (
         outs[0].reshape(48, 32, 512),
         outs[1].reshape(24, 32, 128),
         outs[2].reshape(12, 32, 32),
         outs[3].reshape(6, 32, 64),
-        outs[4].reshape(3, 32, 16),
+        outs[4].reshape(3, 16, 32).transpose(0, 2, 1),
     )
 
 

time: 39.4 us -> 31.2 us (0.79)
  local copies, waits for them, and re-layouts: 8.06 us -> 0 us
    unnamed x15 -> x0, local copies, waits for them, and re-layouts: 8.06 us -> none
    pallas_call x1 -> x2, Pallas kernels: 30.5 us -> 30.4 us  [the longest x1 29.1 us: shards(): pl.pallas_call(kernel, name='blend', out_shape=shapes, in_specs=[hbm] * 5...]
where the time goes in v2:
time: 31.2 us; the launch traced here: 31.1 us
  Pallas kernels  30.4 us (97%)
  between operations  0.64 us (2%)
    pallas_call x1, Pallas kernels, shards(): pl.pallas_call(kernel, name='blend', out_shape=shapes, in_specs=[hbm] * 5...  29.1 us
    pallas_call x1, Pallas kernels, shards(): pl.pallas_call(store, name='store', out_shape=shapes, in_specs=[pl.BlockS...  1.28 us

profile of v2, /device:TPU:385, one launch (start us, length us, event | category | flops | bytes accessed | tf_op | source)
XLA Modules:
  0.0 31.1 jit_solution(8273774767927879904)
XLA Ops:
  0.6 29.1 %blend.1 = (bf16[6,256,512]{2,1,0:T(8,128)(2,1)S(1)}, bf16[6,128,128]{2,1,0:T(8,128)(2,1)S(1)}, bf16[384,32]{1,0:T(8,128)(2,1)S(1)}, bf16[192,64]{1,0:T(8,128)(2,1)S(1)}, bf16[48,32]{1,0:T(8,128)(2,1)S(1)}) custom-call(bf16[7,256,640]{2,1,0:T(8,128)(2,1)} %bitcast.9, s32[56]{0:T(128)} %weight_x_in.1, s32[40]{0:T(128)} %weight_y_in.1, ...), custom_call_target="tpu_custom_call" | custom-call | tf_op jit(solution)/shard_map/blend/pallas_call | solution.py:409
  29.8 1.3 %store.1 = (bf16[6,256,512]{2,1,0:T(8,128)(2,1)}, bf16[6,128,128]{2,1,0:T(8,128)(2,1)}, bf16[384,32]{1,0:T(8,128)(2,1)}, bf16[192,64]{1,0:T(8,128)(2,1)}, bf16[48,32]{1,0:T(8,128)(2,1)}) custom-call(bf16[6,256,512]{2,1,0:T(8,128)(2,1)S(1)} %get-tuple-element.15.refs_0_, bf16[6,128,128]{2,1,0:T(8,128)(2,1)S(1)} %get-tuple-element.16.refs_1_, ...), custom_call_target="tpu_custom_call" | custom-call | tf_op jit(solution)/shard_map/store/pallas_call | solution.py:466

commit v3 on v2

--- a/solution.py
+++ b/solution.py
@@ -12,7 +12,8 @@
 CHUNKS = 6
 ROWS = 256
 PIECES = ((1, 0), (1, 1), (2, 0), (2, 1), (3, 0), (3, 1), (0, 0), (0, 1))
-WAYS = (2, -2, 2, -2, -2, -2, 2, -2, 2)
+POOLED = 8
+VIA = (0, 0, 0, 1, 1, None, None, None, None)
 
 
 def iota(shape, dim):
@@ -54,16 +55,16 @@
     corner_in,
     x_out,
     x_in,
-    xw_out,
-    xw_in,
+    pooled_out,
+    pooled_in,
     relay,
-    relay_w,
     first_y,
     shares,
     pool1,
     pool2,
     pool3,
     pool4,
+    pool_row,
     own_third,
     all_third,
     load_sem,
@@ -86,27 +87,29 @@
     has_left = gx > 0
     has_up = gy > 0
     has_down = gy < 7
-
-    def carries(way):
-        source = (y - way + 8) % 8
-        last = jnp.logical_and(z == 7, source >= 4)
-        return jnp.logical_and(x == 0, jnp.logical_not(last))
-
-    def carry_to(way):
-        source = (y - way + 8) % 8
-        return device(0, (source + 4) % 8, z + source // 4, core)
-
     far_in = jnp.logical_and(x == 0, has_left)
-
+    passing = jnp.logical_not(jnp.logical_and(z == 7, y >= 4))
+
+    def carries(via):
+        return jnp.logical_and(x == via, passing)
+
+    names = (
+        (conv_in, conv),
+        (bias_in, bias),
+        (weight_x_in, weight_x),
+        (weight_y_in, weight_y),
+    )
     loads = [
         pltpu.make_async_copy(features.at[i], held.at[i], load_sem.at[i])
         for i in range(7)
     ]
-    loads.append(pltpu.make_async_copy(conv_in, conv, load_sem.at[7]))
-    loads.append(pltpu.make_async_copy(bias_in, bias, load_sem.at[8]))
-    loads.append(pltpu.make_async_copy(weight_x_in, weight_x, load_sem.at[9]))
-    loads.append(pltpu.make_async_copy(weight_y_in, weight_y, load_sem.at[10]))
-    for i in (7, 8, 9, 10, 6, 0, 1, 2, 3, 4, 5):
+    small = [
+        pltpu.make_async_copy(src, dst, load_sem.at[7 + i])
+        for i, (src, dst) in enumerate(names)
+    ]
+    for copy in small:
+        copy.start()
+    for i in (6, 0, 1, 2, 3, 4, 5):
         loads[i].start()
 
     barrier = pltpu.get_barrier_semaphore()
@@ -114,26 +117,27 @@
     def greet(target):
         pl.semaphore_signal(barrier, inc=1, device_id=target, device_id_type=MESH)
 
-    for way in (2, -2):
-
-        @pl.when(carries(way))
+    @pl.when(far_in)
+    def _():
+        before = z - jnp.where(y < 4, 1, 0)
+        for via in (0, 1):
+            greet(device(via, (y + 4) % 8, before, core))
+
+    @pl.when(has_left)
+    def _():
+        greet((gx - 1, gy))
+
+    for via in (0, 1):
+
+        @pl.when(carries(via))
         def _():
-            greet(device(3, (y - way + 8) % 8, z, core))
-
-        @pl.when(far_in)
-        def _():
-            before = z - jnp.where(y < 4, 1, 0)
-            greet(device(0, (y + 4 + way) % 8, before, core))
-
-    @pl.when(jnp.logical_and(has_left, x > 0))
-    def _():
-        greet((gx - 1, gy))
+            greet(device(3, y, z, core))
 
     for o in range(1, 8):
         greet((gx, (gy + o) % 8))
 
-    for i in (7, 8, 9, 10):
-        loads[i].wait()
+    for copy in small:
+        copy.wait()
 
     pick = (iota((ROWS, 32), 0) % 32) == iota((ROWS, 32), 1)
     spread = one_hot(pick, 1.0)
@@ -151,17 +155,19 @@
 
     lane_y = iota((8, 128), 1) // 16
     row = iota((8, 128), 0)
-    wy_own = jnp.zeros((8, 128), F32)
-    wy_last = jnp.zeros((8, 128), F32)
-    wx_own = jnp.zeros((8, 128), F32)
-    wx_last = jnp.zeros((8, 128), F32)
+    nothing = jnp.zeros((8, 128), F32)
+    wy_own, wy_last, wx_own, wx_last, wx_own_lane, wx_last_lane = (nothing,) * 6
     for k in range(8):
-        wy_own = jnp.where(lane_y == k, weight_y[k].astype(F32), wy_own)
-        wy_last = jnp.where(lane_y == k, weight_y[32 + k].astype(F32), wy_last)
-        wx_own = jnp.where(row == k, weight_x[k].astype(F32), wx_own)
-        wx_last = jnp.where(row == k, weight_x[48 + k].astype(F32), wx_last)
+        own, last = weight_y[k].astype(F32), weight_y[32 + k].astype(F32)
+        wy_own = jnp.where(lane_y == k, own, wy_own)
+        wy_last = jnp.where(lane_y == k, last, wy_last)
+        own, last = weight_x[k].astype(F32), weight_x[48 + k].astype(F32)
+        wx_own = jnp.where(row == k, own, wx_own)
+        wx_last = jnp.where(row == k, last, wx_last)
+        wx_own_lane = jnp.where(lane_y == k, own, wx_own_lane)
+        wx_last_lane = jnp.where(lane_y == k, last, wx_last_lane)
     corner_out[ROWS:, :] = jnp.concatenate([wy_last, wy_last], axis=0).astype(BF16)
-    xw_out[...] = jnp.concatenate([wx_last, wx_last], axis=0).astype(BF16)
+    pooled_out[16:, :] = jnp.concatenate([wx_last, wx_last_lane], axis=0).astype(BF16)
 
     loads[6].wait()
     margin = logits(6)
@@ -169,9 +175,15 @@
     for t in range(4):
         x_out[t] = margin[:, 128 * t : 128 * (t + 1)]
 
-    peers = 7 + near.astype(jnp.int32) + 2 * far.astype(jnp.int32)
-    for way in (2, -2):
-        peers = peers + carries(way).astype(jnp.int32)
+    for i in range(CHUNKS):
+        loads[i].wait()
+        value = logits(i)
+        y_out[i] = value[:, 512:]
+        out0[i] = value[:, :512]
+
+    peers = 7 + near.astype(jnp.int32) + 3 * far.astype(jnp.int32)
+    for via in (0, 1):
+        peers = peers + carries(via).astype(jnp.int32)
     pl.semaphore_wait(barrier, peers)
 
     def remote(src, dst, send, recv, target):
@@ -197,18 +209,23 @@
 
     def direct(h):
         target = ((gx + 1) % 64, gy)
-        src, dst = (xw_out, xw_in) if h == 8 else (part(x_out, h), part(x_in, h))
+        if h == POOLED:
+            src, dst = pooled_out, pooled_in
+        else:
+            src, dst = part(x_out, h), part(x_in, h)
         return remote(src, dst, x_send.at[h], x_recv.at[h], target)
 
     def hop(h):
-        target = device(0, (y + WAYS[h] + 8) % 8, z, core)
-        src, dst = (xw_out, relay_w) if h == 8 else (part(x_out, h), relay.at[h])
-        return remote(src, dst, hop_send.at[h], hop_recv.at[h], target)
+        target = device(VIA[h], y, z, core)
+        return remote(
+            part(x_out, h), relay.at[h], hop_send.at[h], hop_recv.at[h], target
+        )
 
     def onward(h):
-        target = carry_to(WAYS[h])
-        src, dst = (relay_w, xw_in) if h == 8 else (relay.at[h], part(x_in, h))
-        return remote(src, dst, on_send.at[h], x_recv.at[h], target)
+        target = device(0, (y + 4) % 8, z + y // 4, core)
+        return remote(
+            relay.at[h], part(x_in, h), on_send.at[h], x_recv.at[h], target
+        )
 
     def send_x(pieces):
         @pl.when(near)
@@ -219,72 +236,84 @@
         @pl.when(far)
         def _():
             for h in pieces:
-                hop(h).start()
+                (direct if VIA[h] is None else hop)(h).start()
 
     @pl.when(has_down)
     def _():
         corner_copy.start()
 
-    send_x((8, 0, 1, 2, 3, 4, 5))
-
-    for i in range(CHUNKS):
-        loads[i].wait()
-        value = logits(i)
-        y_out[i] = value[:, 512:]
-        out0[i] = value[:, :512]
-
-        @pl.when(has_down)
-        def _():
+    send_x((0, 1, 2, 3, 4, 5))
+
+    @pl.when(has_down)
+    def _():
+        for i in (1, 2, 3, 4, 5, 0):
             y_copies[i].start()
-
-        if i == 3:
-            @pl.when(has_up)
-            def _():
-                corner_copy.wait_recv()
-                wy_up = corner_in[ROWS:, :].astype(F32)[:8]
-                total = wy_own + wy_up
-                own_share, up_share = wy_own / total, wy_up / total
-                shares[0] = own_share
-                shares[1] = up_share
-                x_out[0] = (
-                    x_out[0].astype(F32) * own_share[:1]
-                    + corner_in[:ROWS, :].astype(F32) * up_share[:1]
-                ).astype(BF16)
-
-            send_x((6, 7))
 
     source, target = iota((512, 128), 0), iota((512, 128), 1)
     pool1[...] = one_hot(source // 32 * 8 + source % 16 // 2 == target, 0.125)
+    pool_row[...] = one_hot(
+        source // 128 * 2 + source % 16 // 8 == target % 8, 1.0 / 512
+    )
     source, target = iota((128, 128), 0), iota((128, 128), 1)
     pool2[...] = one_hot(source // 16 * 4 + source % 8 // 2 == target, 0.125)
+    pool4[...] = one_hot(jnp.logical_and(source // 4 == target, source < 64), 0.125)
     pool3[...] = one_hot(
-        jnp.logical_and(
-            source // 8 * 2 + source % 4 // 2 + gy * 8 == target, source < 32
-        ),
+        jnp.logical_and(source // 8 * 2 + source % 4 // 2 == target % 8, source < 32),
         0.125,
     )
-    pool4[...] = one_hot(jnp.logical_and(source // 4 == target, source < 64), 0.125)
-
-    for h in (8, 0, 1, 2, 3, 4, 5, 6, 7):
-
-        @pl.when(carries(WAYS[h]))
+
+    for via in (0, 1):
+
+        @pl.when(carries(via))
         def _():
-            hop(h).wait_recv()
-            onward(h).start()
+            for h in range(9):
+                if VIA[h] == via:
+                    hop(h).wait_recv()
+                    onward(h).start()
+
+    @pl.when(has_up)
+    def _():
+        corner_copy.wait_recv()
+        wy_up = corner_in[ROWS:, :].astype(F32)[:8]
+        total = wy_own + wy_up
+        own_share, up_share = wy_own / total, wy_up / total
+        shares[0] = own_share
+        shares[1] = up_share
+        x_out[0] = (
+            x_out[0].astype(F32) * own_share[:1]
+            + corner_in[:ROWS, :].astype(F32) * up_share[:1]
+        ).astype(BF16)
+
+    group = iota((16, 128), 1) // 8
+
+    def pool_rows(tiles):
+        total = dot(tiles[0], pool_row[:128])
+        for t in range(1, 4):
+            total = total + dot(tiles[t], pool_row[128 * t : 128 * (t + 1)])
+        return total
+
+    send_x((6, 7))
+    rows = pool_rows([x_out[t] for t in range(4)])
+    value = jnp.zeros((16, 128), F32)
+    for g in range(16):
+        value = jnp.where(group == g, rows[16 * g : 16 * (g + 1)], value)
+    pooled_out[:16, :] = value.astype(BF16)
+    send_x((POOLED,))
 
     third = jnp.zeros((16, 128), F32)
 
-    def mips(i, third):
+    def place(third, i, value):
+        third = jnp.where(group == (gy + i) % 16, value[:16], third)
+        return jnp.where(group == (gy + 6 + i) % 16, value[16:], third)
+
+    def mips(i):
         pooled = dot(out0[i], pool1[...]).reshape(4, 2, 32, 128)
         first = (pooled[:, 0] + pooled[:, 1]).astype(BF16).reshape(128, 128)
         out1[i] = first
         pooled = dot(first, pool2[...]).reshape(2, 2, 32, 128)
         second = (pooled[:, 0] + pooled[:, 1]).astype(BF16).reshape(64, 128)
         level2[pl.ds(64 * i, 64), :] = second[:, :32]
-        pooled = dot(second, pool3[...])
-        pooled = pooled[:32] + pooled[32:]
-        third = third + pltpu.roll(pooled[:16], 8 * i, 1)
-        return third + pltpu.roll(pooled[16:], 8 * (6 + i), 1)
+        return second
 
     for i in range(1, CHUNKS):
 
@@ -296,7 +325,8 @@
                 + y_in[i].astype(F32) * shares[1, :1]
             ).astype(BF16)
 
-        third = mips(i, third)
+        pooled = dot(mips(i), pool3[...])
+        third = place(third, i, pooled[:32] + pooled[32:])
 
     first_y[...] = out0[0, :, :128].astype(F32)
 
@@ -305,26 +335,34 @@
         y_copies[0].wait_recv()
         first_y[...] = first_y[...] * shares[0, :1] + y_in[0].astype(F32) * shares[1, :1]
 
-    out0[0, :, :128] = first_y[...].astype(BF16)
-
     @pl.when(has_left)
     def _():
-        for h in (8, 0, 1, 2, 3, 4, 5, 6, 7):
-            direct(h).wait_recv()
-        wx_left = xw_in[...].astype(F32)[:8]
-        total = wx_own + wx_left
-        own_share, left_share = wx_own / total, wx_left / total
-        for a in range(8):
-            rows = pl.ds(32 * a, 32)
-            mine, theirs = own_share[a : a + 1], left_share[a : a + 1]
-            for t in range(4):
-                lanes = pl.ds(128 * t, 128)
-                own = first_y[rows, :] if t == 0 else out0[0, rows, lanes].astype(F32)
-                out0[0, rows, lanes] = (
-                    own * mine + x_in[t, rows, :].astype(F32) * theirs
-                ).astype(BF16)
-
-    third = mips(0, third)
+        direct(POOLED).wait_recv()
+
+    @pl.when(jnp.logical_not(has_left))
+    def _():
+        pooled_in[...] = jnp.zeros((32, 128), BF16)
+
+    left = pooled_in[...].astype(F32)
+    wx_left, wx_left_lane = left[16:24], left[24:]
+    own_share = wx_own / (wx_own + wx_left)
+    left_share = wx_left / (wx_own + wx_left)
+    rows = pool_rows(
+        [first_y[...].astype(BF16)]
+        + [out0[0, :, 128 * t : 128 * (t + 1)] for t in range(1, 4)]
+    )
+    value = jnp.zeros((32, 128), F32)
+    for a in range(8):
+        value = value + rows[32 * a : 32 * (a + 1)] * own_share[a : a + 1]
+    other = left[:16] * (wx_left_lane / (wx_own_lane + wx_left_lane))[:1]
+    for shift in (64, 32, 16):
+        other = other + pltpu.roll(other, shift, 1)
+    turned = pltpu.roll(other, 8, 1)
+    even = group % 2 == 0
+    other = jnp.concatenate(
+        [jnp.where(even, other, turned), jnp.where(even, turned, other)], axis=0
+    )
+    third = place(third, 0, value + other)
 
     own_third[...] = third.astype(BF16)
     third_copies = [
@@ -339,9 +377,29 @@
     ]
     for copy in third_copies:
         copy.start()
+
+    @pl.when(jnp.logical_not(has_left))
+    def _():
+        out0[0, :, :128] = first_y[...].astype(BF16)
+
+    @pl.when(has_left)
+    def _():
+        for h in range(8):
+            direct(h).wait_recv()
+        for a in range(8):
+            rows = pl.ds(32 * a, 32)
+            mine, theirs = own_share[a : a + 1], left_share[a : a + 1]
+            for t in range(4):
+                lanes = pl.ds(128 * t, 128)
+                own = first_y[rows, :] if t == 0 else out0[0, rows, lanes].astype(F32)
+                out0[0, rows, lanes] = (
+                    own * mine + x_in[t, rows, :].astype(F32) * theirs
+                ).astype(BF16)
+
+    mips(0)
+
     for copy in third_copies:
         copy.wait_recv()
-    group = iota((16, 128), 1) // 8
     parts = [own_third[...].astype(F32)] + [
         all_third[o].astype(F32) for o in range(1, 8)
     ]
@@ -377,13 +435,15 @@
     @pl.when(far)
     def _():
         for h in range(9):
-            hop(h).wait_send()
-
-    for h in range(9):
-
-        @pl.when(carries(WAYS[h]))
+            (direct if VIA[h] is None else hop)(h).wait_send()
+
+    for via in (0, 1):
+
+        @pl.when(carries(via))
         def _():
-            onward(h).wait_send()
+            for h in range(9):
+                if VIA[h] == via:
+                    onward(h).wait_send()
 
 
 def store(*refs):
@@ -425,16 +485,16 @@
             pltpu.VMEM((272, 128), BF16),
             pltpu.VMEM((4, 256, 128), BF16),
             pltpu.VMEM((4, 256, 128), BF16),
-            pltpu.VMEM((16, 128), BF16),
-            pltpu.VMEM((16, 128), BF16),
-            pltpu.VMEM((8, 128, 128), BF16),
-            pltpu.VMEM((16, 128), BF16),
+            pltpu.VMEM((32, 128), BF16),
+            pltpu.VMEM((32, 128), BF16),
+            pltpu.VMEM((5, 128, 128), BF16),
             pltpu.VMEM((256, 128), F32),
             pltpu.VMEM((2, 8, 128), F32),
             pltpu.VMEM((512, 128), BF16),
             pltpu.VMEM((128, 128), BF16),
             pltpu.VMEM((128, 128), BF16),
             pltpu.VMEM((128, 128), BF16),
+            pltpu.VMEM((512, 128), BF16),
             pltpu.VMEM((16, 128), BF16),
             pltpu.VMEM((8, 16, 128), BF16),
             dma((11,)),
@@ -442,9 +502,9 @@
             dma((7,)),
             dma((9,)),
             dma((9,)),
-            dma((9,)),
-            dma((9,)),
-            dma((9,)),
+            dma((5,)),
+            dma((5,)),
+            dma((5,)),
             dma((8,)),
             dma((8,)),
         ],

time: 31.2 us -> 27.4 us (0.88)
  the two profiles are of different devices: /device:TPU:385 before, /device:TPU:257 now
where the time goes in v3:
time: 27.4 us; the launch traced here: 27.3 us
  Pallas kernels  26.7 us (97%)
  between operations  0.64 us (2%)
    pallas_call x1, Pallas kernels, shards(): pl.pallas_call(kernel, name='blend', out_shape=shapes, in_specs=[hbm] * 5...  25.4 us
    pallas_call x1, Pallas kernels, shards(): pl.pallas_call(store, name='store', out_shape=shapes, in_specs=[pl.BlockS...  1.28 us

profile of v3, /device:TPU:257, one launch (start us, length us, event | category | flops | bytes accessed | tf_op | source)
XLA Modules:
  0.0 27.3 jit_solution(14600992032980382707)
XLA Ops:
  0.6 25.4 %blend.1 = (bf16[6,256,512]{2,1,0:T(8,128)(2,1)S(1)}, bf16[6,128,128]{2,1,0:T(8,128)(2,1)S(1)}, bf16[384,32]{1,0:T(8,128)(2,1)S(1)}, bf16[192,64]{1,0:T(8,128)(2,1)S(1)}, bf16[48,32]{1,0:T(8,128)(2,1)S(1)}) custom-call(bf16[7,256,640]{2,1,0:T(8,128)(2,1)} %bitcast.9, s32[56]{0:T(128)} %weight_x_in.1, s32[40]{0:T(128)} %weight_y_in.1, ...), custom_call_target="tpu_custom_call" | custom-call | tf_op jit(solution)/shard_map/blend/pallas_call | solution.py:469
  26.0 1.3 %store.1 = (bf16[6,256,512]{2,1,0:T(8,128)(2,1)}, bf16[6,128,128]{2,1,0:T(8,128)(2,1)}, bf16[384,32]{1,0:T(8,128)(2,1)}, bf16[192,64]{1,0:T(8,128)(2,1)}, bf16[48,32]{1,0:T(8,128)(2,1)}) custom-call(bf16[6,256,512]{2,1,0:T(8,128)(2,1)S(1)} %get-tuple-element.15.refs_0_, bf16[6,128,128]{2,1,0:T(8,128)(2,1)S(1)} %get-tuple-element.16.refs_1_, ...), custom_call_target="tpu_custom_call" | custom-call | tf_op jit(solution)/shard_map/store/pallas_call | solution.py:526

commit v4 on v3

--- a/solution.py
+++ b/solution.py
@@ -77,6 +77,7 @@
     on_send,
     third_send,
     third_recv,
+    told,
 ):
     gx = lax.axis_index("gx")
     gy = lax.axis_index("gy")
@@ -114,27 +115,46 @@
 
     barrier = pltpu.get_barrier_semaphore()
 
-    def greet(target):
-        pl.semaphore_signal(barrier, inc=1, device_id=target, device_id_type=MESH)
+    def tell(semaphore, target):
+        pl.semaphore_signal(semaphore, inc=1, device_id=target, device_id_type=MESH)
+
+    middle_y = (y + 6) % 8
+    middle = jnp.logical_and(
+        x == 0, jnp.logical_not(jnp.logical_and(z == 7, middle_y >= 4))
+    )
+
+    for via in (0, 1):
+
+        @pl.when(carries(via))
+        def _():
+            tell(barrier, device(3, y, z, core))
+            tell(barrier, device(0, (y + 2) % 8, z, core))
+
+    @pl.when(far)
+    def _():
+        tell(barrier, device(0, (y + 2) % 8, z, core))
 
     @pl.when(far_in)
     def _():
-        before = z - jnp.where(y < 4, 1, 0)
-        for via in (0, 1):
-            greet(device(via, (y + 4) % 8, before, core))
-
-    @pl.when(has_left)
-    def _():
-        greet((gx - 1, gy))
-
-    for via in (0, 1):
-
-        @pl.when(carries(via))
-        def _():
-            greet(device(3, y, z, core))
-
-    for o in range(1, 8):
-        greet((gx, (gy + o) % 8))
+        tell(barrier, device(0, middle_y, z - jnp.where(y < 4, 1, 0), core))
+
+    @pl.when(x > 0)
+    def _():
+        tell(barrier, (gx - 1, gy))
+
+    def tell_group(semaphore, steps):
+        @pl.when(gy >= steps)
+        def _():
+            tell(semaphore, (gx, gy - steps))
+
+        @pl.when(gy + steps < 8)
+        def _():
+            tell(semaphore, (gx, gy + steps))
+
+    def in_group(steps):
+        return (gy >= steps).astype(jnp.int32) + (gy + steps < 8).astype(jnp.int32)
+
+    tell_group(barrier, 1)
 
     for copy in small:
         copy.wait()
@@ -150,8 +170,8 @@
     block[...] = jnp.where(same, wide, 0.0).astype(BF16)
     bias_column = jnp.sum(jnp.where(pick, bias[...], 0.0), axis=1, keepdims=True)
 
-    def logits(i):
-        return (dot(block[...], held[i]) + bias_column).astype(BF16)
+    def logits(i, lanes):
+        return (dot(block[...], held[i, :, lanes]) + bias_column).astype(BF16)
 
     lane_y = iota((8, 128), 1) // 16
     row = iota((8, 128), 0)
@@ -170,21 +190,25 @@
     pooled_out[16:, :] = jnp.concatenate([wx_last, wx_last_lane], axis=0).astype(BF16)
 
     loads[6].wait()
-    margin = logits(6)
+    margin = logits(6, slice(0, 640))
     corner_out[:ROWS, :] = margin[:, 512:]
     for t in range(4):
         x_out[t] = margin[:, 128 * t : 128 * (t + 1)]
 
     for i in range(CHUNKS):
         loads[i].wait()
-        value = logits(i)
-        y_out[i] = value[:, 512:]
-        out0[i] = value[:, :512]
-
-    peers = 7 + near.astype(jnp.int32) + 3 * far.astype(jnp.int32)
-    for via in (0, 1):
-        peers = peers + carries(via).astype(jnp.int32)
+        y_out[i] = logits(i, slice(512, 640))
+
+    peers = in_group(1) + near.astype(jnp.int32)
+    peers = peers + 2 * far.astype(jnp.int32) + 4 * middle.astype(jnp.int32)
     pl.semaphore_wait(barrier, peers)
+
+    @pl.when(middle)
+    def _():
+        for source_x in (0, 1, 3):
+            tell(told.at[0], device(source_x, middle_y, z, core))
+
+    tell_group(told.at[1], 1)
 
     def remote(src, dst, send, recv, target):
         return pltpu.make_async_remote_copy(
@@ -242,12 +266,18 @@
     def _():
         corner_copy.start()
 
-    send_x((0, 1, 2, 3, 4, 5))
+    send_x((0, 1, 2, 3, 4))
 
     @pl.when(has_down)
     def _():
         for i in (1, 2, 3, 4, 5, 0):
             y_copies[i].start()
+
+    for i in range(CHUNKS):
+        out0[i] = logits(i, slice(0, 512))
+
+    pl.semaphore_wait(told.at[1], in_group(1))
+    tell_group(told.at[2], 2)
 
     source, target = iota((512, 128), 0), iota((512, 128), 1)
     pool1[...] = one_hot(source // 32 * 8 + source % 16 // 2 == target, 0.125)
@@ -262,14 +292,27 @@
         0.125,
     )
 
+    @pl.when(far)
+    def _():
+        pl.semaphore_wait(told.at[0], 1)
+
+    send_x((5,))
+
     for via in (0, 1):
 
         @pl.when(carries(via))
         def _():
+            pl.semaphore_wait(told.at[0], 1)
             for h in range(9):
                 if VIA[h] == via:
                     hop(h).wait_recv()
                     onward(h).start()
+
+    def pool_rows(tiles):
+        return sum(dot(v, pool_row[128 * t : 128 * (t + 1)]) for t, v in tiles)
+
+    group = iota((16, 128), 1) // 8
+    rows = pool_rows([(t, x_out[t]) for t in range(1, 4)])
 
     @pl.when(has_up)
     def _():
@@ -284,21 +327,15 @@
             + corner_in[:ROWS, :].astype(F32) * up_share[:1]
         ).astype(BF16)
 
-    group = iota((16, 128), 1) // 8
-
-    def pool_rows(tiles):
-        total = dot(tiles[0], pool_row[:128])
-        for t in range(1, 4):
-            total = total + dot(tiles[t], pool_row[128 * t : 128 * (t + 1)])
-        return total
-
-    send_x((6, 7))
-    rows = pool_rows([x_out[t] for t in range(4)])
+    rows = rows + pool_rows([(0, x_out[0])])
     value = jnp.zeros((16, 128), F32)
     for g in range(16):
         value = jnp.where(group == g, rows[16 * g : 16 * (g + 1)], value)
     pooled_out[:16, :] = value.astype(BF16)
-    send_x((POOLED,))
+    send_x((POOLED, 6, 7))
+
+    pl.semaphore_wait(told.at[2], in_group(2))
+    tell_group(told.at[3], 4)
 
     third = jnp.zeros((16, 128), F32)
 
@@ -348,8 +385,8 @@
     own_share = wx_own / (wx_own + wx_left)
     left_share = wx_left / (wx_own + wx_left)
     rows = pool_rows(
-        [first_y[...].astype(BF16)]
-        + [out0[0, :, 128 * t : 128 * (t + 1)] for t in range(1, 4)]
+        [(0, first_y[...].astype(BF16))]
+        + [(t, out0[0, :, 128 * t : 128 * (t + 1)]) for t in range(1, 4)]
     )
     value = jnp.zeros((32, 128), F32)
     for a in range(8):
@@ -364,6 +401,7 @@
     )
     third = place(third, 0, value + other)
 
+    pl.semaphore_wait(told.at[3], 1)
     own_third[...] = third.astype(BF16)
     third_copies = [
         remote(
@@ -507,6 +545,7 @@
             dma((5,)),
             dma((8,)),
             dma((8,)),
+            pltpu.SemaphoreType.REGULAR((4,)),
         ],
         compiler_params=pltpu.CompilerParams(
             collective_id=0, has_side_effects=True, vmem_limit_bytes=24 << 20

time: 27.4 us -> 25 us (0.912)
  the two profiles are of different devices: /device:TPU:257 before, /device:TPU:449 now
where the time goes in v4:
time: 25 us; the launch traced here: 24.9 us
  Pallas kernels  24.2 us (97%)
  between operations  0.64 us (3%)
    pallas_call x1, Pallas kernels, shards(): pl.pallas_call(kernel, name='blend', out_shape=shapes, in_specs=[hbm] * 5...  22.9 us
    pallas_call x1, Pallas kernels, shards(): pl.pallas_call(store, name='store', out_shape=shapes, in_specs=[pl.BlockS...  1.28 us

profile of v4, /device:TPU:449, one launch (start us, length us, event | category | flops | bytes accessed | tf_op | source)
XLA Modules:
  0.0 24.9 jit_solution(15691756055208560770)
XLA Ops:
  0.6 22.9 %blend.1 = (bf16[6,256,512]{2,1,0:T(8,128)(2,1)S(1)}, bf16[6,128,128]{2,1,0:T(8,128)(2,1)S(1)}, bf16[384,32]{1,0:T(8,128)(2,1)S(1)}, bf16[192,64]{1,0:T(8,128)(2,1)S(1)}, bf16[48,32]{1,0:T(8,128)(2,1)S(1)}) custom-call(bf16[7,256,640]{2,1,0:T(8,128)(2,1)} %bitcast.9, s32[56]{0:T(128)} %weight_x_in.1, s32[40]{0:T(128)} %weight_y_in.1, ...), custom_call_target="tpu_custom_call" | custom-call | tf_op jit(solution)/shard_map/blend/pallas_call | solution.py:507
  23.6 1.3 %store.1 = (bf16[6,256,512]{2,1,0:T(8,128)(2,1)}, bf16[6,128,128]{2,1,0:T(8,128)(2,1)}, bf16[384,32]{1,0:T(8,128)(2,1)}, bf16[192,64]{1,0:T(8,128)(2,1)}, bf16[48,32]{1,0:T(8,128)(2,1)}) custom-call(bf16[6,256,512]{2,1,0:T(8,128)(2,1)S(1)} %get-tuple-element.15.refs_0_, bf16[6,128,128]{2,1,0:T(8,128)(2,1)S(1)} %get-tuple-element.16.refs_1_, ...), custom_call_target="tpu_custom_call" | custom-call | tf_op jit(solution)/shard_map/store/pallas_call | solution.py:565

commit v5 on v4

--- a/solution.py
+++ b/solution.py
@@ -13,7 +13,7 @@
 ROWS = 256
 PIECES = ((1, 0), (1, 1), (2, 0), (2, 1), (3, 0), (3, 1), (0, 0), (0, 1))
 POOLED = 8
-VIA = (0, 0, 0, 1, 1, None, None, None, None)
+VIA = (0, 0, 1, 1, 2, 2, None, None, None)
 
 
 def iota(shape, dim):
@@ -67,6 +67,8 @@
     pool_row,
     own_third,
     all_third,
+    own_first,
+    all_first,
     load_sem,
     y_send,
     y_recv,
@@ -108,9 +110,11 @@
         pltpu.make_async_copy(src, dst, load_sem.at[7 + i])
         for i, (src, dst) in enumerate(names)
     ]
-    for copy in small:
+    small[0].start()
+    loads[6].start()
+    for copy in small[1:]:
         copy.start()
-    for i in (6, 0, 1, 2, 3, 4, 5):
+    for i in range(CHUNKS):
         loads[i].start()
 
     barrier = pltpu.get_barrier_semaphore()
@@ -118,25 +122,24 @@
     def tell(semaphore, target):
         pl.semaphore_signal(semaphore, inc=1, device_id=target, device_id_type=MESH)
 
-    middle_y = (y + 6) % 8
-    middle = jnp.logical_and(
-        x == 0, jnp.logical_not(jnp.logical_and(z == 7, middle_y >= 4))
-    )
-
-    for via in (0, 1):
+    middle = jnp.logical_and(x == 2, passing)
+
+    for via in (0, 1, 2):
 
         @pl.when(carries(via))
         def _():
             tell(barrier, device(3, y, z, core))
-            tell(barrier, device(0, (y + 2) % 8, z, core))
+            if via != 2:
+                tell(barrier, device(2, y, z, core))
 
     @pl.when(far)
     def _():
-        tell(barrier, device(0, (y + 2) % 8, z, core))
+        tell(barrier, device(2, y, z, core))
 
     @pl.when(far_in)
     def _():
-        tell(barrier, device(0, middle_y, z - jnp.where(y < 4, 1, 0), core))
+        before = z - jnp.where(y < 4, 1, 0)
+        tell(barrier, device(2, (y + 4) % 8, before, core))
 
     @pl.when(x > 0)
     def _():
@@ -159,16 +162,17 @@
     for copy in small:
         copy.wait()
 
-    pick = (iota((ROWS, 32), 0) % 32) == iota((ROWS, 32), 1)
-    spread = one_hot(pick, 1.0)
-    dims = (((1,), (1,)), ((), ()))
-    tall = lax.dot_general(spread, conv[...], dims, preferred_element_type=F32)
-    wide = lax.dot_general(
-        tall.astype(BF16), spread, dims, preferred_element_type=F32
-    )
-    same = iota((ROWS, ROWS), 0) // 32 == iota((ROWS, ROWS), 1) // 32
-    block[...] = jnp.where(same, wide, 0.0).astype(BF16)
-    bias_column = jnp.sum(jnp.where(pick, bias[...], 0.0), axis=1, keepdims=True)
+    table = jnp.concatenate(
+        [conv[...].astype(F32), jnp.broadcast_to(bias[...], (8, 32))], axis=0
+    )
+    table = jnp.concatenate([table, jnp.zeros((40, 96), F32)], axis=1).T[:32]
+    wide = jnp.concatenate([table[:, :32]] * 4, axis=1)
+    tall = jnp.concatenate([wide] * 8, axis=0)
+    for t in range(2):
+        columns = iota((ROWS, 128), 1) + 128 * t
+        same = iota((ROWS, 128), 0) // 32 == columns // 32
+        block[:, 128 * t : 128 * (t + 1)] = jnp.where(same, tall, 0.0).astype(BF16)
+    bias_column = jnp.concatenate([table[:, 32:33]] * 8, axis=0)
 
     def logits(i, lanes):
         return (dot(block[...], held[i, :, lanes]) + bias_column).astype(BF16)
@@ -190,23 +194,16 @@
     pooled_out[16:, :] = jnp.concatenate([wx_last, wx_last_lane], axis=0).astype(BF16)
 
     loads[6].wait()
-    margin = logits(6, slice(0, 640))
-    corner_out[:ROWS, :] = margin[:, 512:]
-    for t in range(4):
-        x_out[t] = margin[:, 128 * t : 128 * (t + 1)]
-
-    for i in range(CHUNKS):
-        loads[i].wait()
-        y_out[i] = logits(i, slice(512, 640))
+    corner_out[:ROWS, :] = logits(6, slice(512, 640))
 
     peers = in_group(1) + near.astype(jnp.int32)
-    peers = peers + 2 * far.astype(jnp.int32) + 4 * middle.astype(jnp.int32)
+    peers = peers + 3 * far.astype(jnp.int32) + 4 * middle.astype(jnp.int32)
     pl.semaphore_wait(barrier, peers)
 
     @pl.when(middle)
     def _():
-        for source_x in (0, 1, 3):
-            tell(told.at[0], device(source_x, middle_y, z, core))
+        for source_x in (3, 0, 1):
+            tell(told.at[0], device(source_x, y, z, core))
 
     tell_group(told.at[1], 1)
 
@@ -266,11 +263,18 @@
     def _():
         corner_copy.start()
 
-    send_x((0, 1, 2, 3, 4))
-
-    @pl.when(has_down)
-    def _():
-        for i in (1, 2, 3, 4, 5, 0):
+    margin = logits(6, slice(0, 512))
+    for t in range(4):
+        x_out[t] = margin[:, 128 * t : 128 * (t + 1)]
+
+    send_x((0, 1, 2, 3, 4, 5))
+
+    for i in (1, 2, 3, 4, 5, 0):
+        loads[i].wait()
+        y_out[i] = logits(i, slice(512, 640))
+
+        @pl.when(has_down)
+        def _():
             y_copies[i].start()
 
     for i in range(CHUNKS):
@@ -296,13 +300,13 @@
     def _():
         pl.semaphore_wait(told.at[0], 1)
 
-    send_x((5,))
-
-    for via in (0, 1):
+
+    for via in (0, 1, 2):
 
         @pl.when(carries(via))
         def _():
-            pl.semaphore_wait(told.at[0], 1)
+            if via != 2:
+                pl.semaphore_wait(told.at[0], 1)
             for h in range(9):
                 if VIA[h] == via:
                     hop(h).wait_recv()
@@ -343,8 +347,8 @@
         third = jnp.where(group == (gy + i) % 16, value[:16], third)
         return jnp.where(group == (gy + 6 + i) % 16, value[16:], third)
 
-    def mips(i):
-        pooled = dot(out0[i], pool1[...]).reshape(4, 2, 32, 128)
+    def mips(i, pooled):
+        pooled = pooled.reshape(4, 2, 32, 128)
         first = (pooled[:, 0] + pooled[:, 1]).astype(BF16).reshape(128, 128)
         out1[i] = first
         pooled = dot(first, pool2[...]).reshape(2, 2, 32, 128)
@@ -362,8 +366,30 @@
                 + y_in[i].astype(F32) * shares[1, :1]
             ).astype(BF16)
 
-        pooled = dot(mips(i), pool3[...])
+        pooled = dot(mips(i, dot(out0[i], pool1[...])), pool3[...])
         third = place(third, i, pooled[:32] + pooled[32:])
+
+    def gather(own, everyone, first_sem):
+        copies = [
+            remote(
+                own,
+                everyone.at[o],
+                third_send.at[first_sem + o],
+                third_recv.at[first_sem + o],
+                (gx, (gy + o) % 8),
+            )
+            for o in range(1, 8)
+        ]
+        for copy in copies:
+            copy.start()
+        return copies
+
+    def blocks(own, everyone):
+        return [own[...].astype(F32)] + [everyone[o].astype(F32) for o in range(1, 8)]
+
+    pl.semaphore_wait(told.at[3], 1)
+    own_third[...] = third.astype(BF16)
+    third_copies = gather(own_third, all_third, 0)
 
     first_y[...] = out0[0, :, :128].astype(F32)
 
@@ -371,6 +397,11 @@
     def _():
         y_copies[0].wait_recv()
         first_y[...] = first_y[...] * shares[0, :1] + y_in[0].astype(F32) * shares[1, :1]
+
+    rows = pool_rows(
+        [(0, first_y[...].astype(BF16))]
+        + [(t, out0[0, :, 128 * t : 128 * (t + 1)]) for t in range(1, 4)]
+    )
 
     @pl.when(has_left)
     def _():
@@ -384,10 +415,6 @@
     wx_left, wx_left_lane = left[16:24], left[24:]
     own_share = wx_own / (wx_own + wx_left)
     left_share = wx_left / (wx_own + wx_left)
-    rows = pool_rows(
-        [(0, first_y[...].astype(BF16))]
-        + [(t, out0[0, :, 128 * t : 128 * (t + 1)]) for t in range(1, 4)]
-    )
     value = jnp.zeros((32, 128), F32)
     for a in range(8):
         value = value + rows[32 * a : 32 * (a + 1)] * own_share[a : a + 1]
@@ -396,67 +423,69 @@
         other = other + pltpu.roll(other, shift, 1)
     turned = pltpu.roll(other, 8, 1)
     even = group % 2 == 0
-    other = jnp.concatenate(
+    value = value + jnp.concatenate(
         [jnp.where(even, other, turned), jnp.where(even, turned, other)], axis=0
     )
-    third = place(third, 0, value + other)
-
-    pl.semaphore_wait(told.at[3], 1)
-    own_third[...] = third.astype(BF16)
-    third_copies = [
-        remote(
-            own_third,
-            all_third.at[o],
-            third_send.at[o],
-            third_recv.at[o],
-            (gx, (gy + o) % 8),
-        )
-        for o in range(1, 8)
-    ]
-    for copy in third_copies:
-        copy.start()
-
-    @pl.when(jnp.logical_not(has_left))
-    def _():
-        out0[0, :, :128] = first_y[...].astype(BF16)
-
-    @pl.when(has_left)
-    def _():
-        for h in range(8):
-            direct(h).wait_recv()
-        for a in range(8):
-            rows = pl.ds(32 * a, 32)
-            mine, theirs = own_share[a : a + 1], left_share[a : a + 1]
-            for t in range(4):
-                lanes = pl.ds(128 * t, 128)
-                own = first_y[rows, :] if t == 0 else out0[0, rows, lanes].astype(F32)
-                out0[0, rows, lanes] = (
-                    own * mine + x_in[t, rows, :].astype(F32) * theirs
+    own_first[...] = jnp.where(group < 8, value[:16], value[16:]).astype(BF16)
+    first_copies = gather(own_first, all_first, 8)
+
+    pooled = jnp.zeros((ROWS, 128), F32)
+    for t in (1, 2, 3, 0):
+        lanes = slice(128 * t, 128 * (t + 1))
+        if t == 0:
+            for copy in third_copies:
+                copy.wait_recv()
+            parts = blocks(own_third, all_third)
+            rows = []
+            for q in (1, 7, 2, 8, 3, 9, 4, 10, 5, 11):
+                owner = (group - q + 16) % 16
+                value = jnp.zeros((16, 128), F32)
+                for o in range(8):
+                    value = jnp.where(owner == (gy - o + 8) % 8, parts[o], value)
+                rows.append(pltpu.roll(value, 128 - 8 * q, 1))
+            later = jnp.concatenate(rows, axis=0).astype(BF16)
+            level3[32:, :] = later[:, :64]
+            fourth = dot(later[32:], pool4[...]).reshape(2, 2, 32, 128)
+            fourth = fourth[:, 0] + fourth[:, 1]
+            for i in range(2):
+                level4[16 * i + 16 : 16 * i + 32, :] = fourth[i].T[:16].astype(BF16)
+
+            @pl.when(jnp.logical_not(has_left))
+            def _():
+                out0[0, :, :128] = first_y[...].astype(BF16)
+
+        @pl.when(has_left)
+        def _():
+            for h in range(8):
+                if PIECES[h][0] == t:
+                    direct(h).wait_recv()
+            for a in range(8):
+                part_rows = slice(32 * a, 32 * (a + 1))
+                if t == 0:
+                    own = first_y[part_rows, :]
+                else:
+                    own = out0[0, part_rows, lanes].astype(F32)
+                out0[0, part_rows, lanes] = (
+                    own * own_share[a : a + 1]
+                    + x_in[t, part_rows, :].astype(F32) * left_share[a : a + 1]
                 ).astype(BF16)
 
-    mips(0)
-
-    for copy in third_copies:
+        pooled = pooled + dot(out0[0, :, lanes], pool1[lanes, :])
+
+    mips(0, pooled)
+
+    for copy in first_copies:
         copy.wait_recv()
-    parts = [own_third[...].astype(F32)] + [
-        all_third[o].astype(F32) for o in range(1, 8)
-    ]
-    rows = [None] * 12
-    for q in range(12):
-        owner = (group - q + 16) % 16
-        value = jnp.zeros((16, 128), F32)
-        for o in range(8):
-            value = jnp.where(owner == (gy - o + 8) % 8, parts[o], value)
-        half, i = q // 6, q % 6
-        rows[2 * i + half] = pltpu.roll(value, (128 - 8 * q) % 128, 1)
-    whole = jnp.concatenate(rows, axis=0).astype(BF16)
-    level3[...] = whole[:, :64]
-    pooled = dot(whole, pool4[...]).reshape(3, 2, 32, 128)
-    fourth = pooled[:, 0] + pooled[:, 1]
-    for t in range(3):
-        level4[pl.ds(16 * t, 16), :] = fourth[t].T[:16].astype(BF16)
-
-    for copy in third_copies:
+    parts = blocks(own_first, all_first)
+    value = jnp.zeros((16, 128), F32)
+    for o in range(8):
+        value = jnp.where(group % 8 == (gy - o + 8) % 8, parts[o], value)
+    value = jnp.concatenate([value, pltpu.roll(value, 64, 1)], axis=0).astype(BF16)
+    level3[:32, :] = value[:, :64]
+    fourth = dot(value, pool4[...]) + dot(later[:32], pool4[...])
+    level4[:16, :] = fourth.T[:16].astype(BF16)
+
+    for copy in third_copies + first_copies:
         copy.wait_send()
 
     @pl.when(has_down)
@@ -475,7 +504,7 @@
         for h in range(9):
             (direct if VIA[h] is None else hop)(h).wait_send()
 
-    for via in (0, 1):
+    for via in (0, 1, 2):
 
         @pl.when(carries(via))
         def _():
@@ -525,7 +554,7 @@
             pltpu.VMEM((4, 256, 128), BF16),
             pltpu.VMEM((32, 128), BF16),
             pltpu.VMEM((32, 128), BF16),
-            pltpu.VMEM((5, 128, 128), BF16),
+            pltpu.VMEM((6, 128, 128), BF16),
             pltpu.VMEM((256, 128), F32),
             pltpu.VMEM((2, 8, 128), F32),
             pltpu.VMEM((512, 128), BF16),
@@ -535,16 +564,18 @@
             pltpu.VMEM((512, 128), BF16),
             pltpu.VMEM((16, 128), BF16),
             pltpu.VMEM((8, 16, 128), BF16),
+            pltpu.VMEM((16, 128), BF16),
+            pltpu.VMEM((8, 16, 128), BF16),
             dma((11,)),
             dma((7,)),
             dma((7,)),
             dma((9,)),
             dma((9,)),
-            dma((5,)),
-            dma((5,)),
-            dma((5,)),
-            dma((8,)),
-            dma((8,)),
+            dma((6,)),
+            dma((6,)),
+            dma((6,)),
+            dma((16,)),
+            dma((16,)),
             pltpu.SemaphoreType.REGULAR((4,)),
         ],
         compiler_params=pltpu.CompilerParams(

time: 25 us -> 23.4 us (0.936)
  the two profiles are of different devices: /device:TPU:449 before, /device:TPU:273 now
where the time goes in v5:
time: 23.4 us; the launch traced here: 23.2 us
  Pallas kernels  22.6 us (97%)
  between operations  0.64 us (3%)
    pallas_call x1, Pallas kernels, shards(): pl.pallas_call(kernel, name='blend', out_shape=shapes, in_specs=[hbm] * 5...  21.3 us
    pallas_call x1, Pallas kernels, shards(): pl.pallas_call(store, name='store', out_shape=shapes, in_specs=[pl.BlockS...  1.28 us

profile of v5, /device:TPU:273, one launch (start us, length us, event | category | flops | bytes accessed | tf_op | source)
XLA Modules:
  0.0 23.2 jit_solution(13699803367563688517)
XLA Ops:
  0.6 21.3 %blend.1 = (bf16[6,256,512]{2,1,0:T(8,128)(2,1)S(1)}, bf16[6,128,128]{2,1,0:T(8,128)(2,1)S(1)}, bf16[384,32]{1,0:T(8,128)(2,1)S(1)}, bf16[192,64]{1,0:T(8,128)(2,1)S(1)}, bf16[48,32]{1,0:T(8,128)(2,1)S(1)}) custom-call(bf16[7,256,640]{2,1,0:T(8,128)(2,1)} %bitcast.9, s32[56]{0:T(128)} %weight_x_in.1, s32[40]{0:T(128)} %weight_y_in.1, ...), custom_call_target="tpu_custom_call" | custom-call | tf_op jit(solution)/shard_map/blend/pallas_call | solution.py:536
  21.9 1.3 %store.1 = (bf16[6,256,512]{2,1,0:T(8,128)(2,1)}, bf16[6,128,128]{2,1,0:T(8,128)(2,1)}, bf16[384,32]{1,0:T(8,128)(2,1)}, bf16[192,64]{1,0:T(8,128)(2,1)}, bf16[48,32]{1,0:T(8,128)(2,1)}) custom-call(bf16[6,256,512]{2,1,0:T(8,128)(2,1)S(1)} %get-tuple-element.15.refs_0_, bf16[6,128,128]{2,1,0:T(8,128)(2,1)S(1)} %get-tuple-element.16.refs_1_, ...), custom_call_target="tpu_custom_call" | custom-call | tf_op jit(solution)/shard_map/store/pallas_call | solution.py:596

commit v6 on v5

--- a/solution.py
+++ b/solution.py
@@ -13,7 +13,7 @@
 ROWS = 256
 PIECES = ((1, 0), (1, 1), (2, 0), (2, 1), (3, 0), (3, 1), (0, 0), (0, 1))
 POOLED = 8
-VIA = (0, 0, 1, 1, 2, 2, None, None, None)
+VIA = (0, 0, 1, 1, 1, 2, None, None, None)
 
 
 def iota(shape, dim):

time: 23.4 us -> 22.8 us (0.974)
  the two profiles are of different devices: /device:TPU:273 before, /device:TPU:257 now
where the time goes in v6:
time: 22.8 us; the launch traced here: 22.6 us
  Pallas kernels  22 us (96%)
  between operations  0.64 us (3%)
    pallas_call x1, Pallas kernels, shards(): pl.pallas_call(kernel, name='blend', out_shape=shapes, in_specs=[hbm] * 5...  20.7 us
    pallas_call x1, Pallas kernels, shards(): pl.pallas_call(store, name='store', out_shape=shapes, in_specs=[pl.BlockS...  1.28 us

profile of v6, /device:TPU:257, one launch (start us, length us, event | category | flops | bytes accessed | tf_op | source)
XLA Modules:
  0.0 22.6 jit_solution(5771748883787681438)
XLA Ops:
  0.6 20.7 %blend.1 = (bf16[6,256,512]{2,1,0:T(8,128)(2,1)S(1)}, bf16[6,128,128]{2,1,0:T(8,128)(2,1)S(1)}, bf16[384,32]{1,0:T(8,128)(2,1)S(1)}, bf16[192,64]{1,0:T(8,128)(2,1)S(1)}, bf16[48,32]{1,0:T(8,128)(2,1)S(1)}) custom-call(bf16[7,256,640]{2,1,0:T(8,128)(2,1)} %bitcast.9, s32[56]{0:T(128)} %weight_x_in.1, s32[40]{0:T(128)} %weight_y_in.1, ...), custom_call_target="tpu_custom_call" | custom-call | tf_op jit(solution)/shard_map/blend/pallas_call | solution.py:536
  21.3 1.3 %store.1 = (bf16[6,256,512]{2,1,0:T(8,128)(2,1)}, bf16[6,128,128]{2,1,0:T(8,128)(2,1)}, bf16[384,32]{1,0:T(8,128)(2,1)}, bf16[192,64]{1,0:T(8,128)(2,1)}, bf16[48,32]{1,0:T(8,128)(2,1)}) custom-call(bf16[6,256,512]{2,1,0:T(8,128)(2,1)S(1)} %get-tuple-element.15.refs_0_, bf16[6,128,128]{2,1,0:T(8,128)(2,1)S(1)} %get-tuple-element.16.refs_1_, ...), custom_call_target="tpu_custom_call" | custom-call | tf_op jit(solution)/shard_map/store/pallas_call | solution.py:596

commit v7 on v6

--- a/solution.py
+++ b/solution.py
@@ -13,7 +13,7 @@
 ROWS = 256
 PIECES = ((1, 0), (1, 1), (2, 0), (2, 1), (3, 0), (3, 1), (0, 0), (0, 1))
 POOLED = 8
-VIA = (0, 0, 1, 1, 1, 2, None, None, None)
+VIA = (2, 1, 1, 1, 0, 0, None, None, None)
 
 
 def iota(shape, dim):
@@ -269,11 +269,12 @@
 
     send_x((0, 1, 2, 3, 4, 5))
 
+    not_far = jnp.logical_not(far)
     for i in (1, 2, 3, 4, 5, 0):
         loads[i].wait()
         y_out[i] = logits(i, slice(512, 640))
 
-        @pl.when(has_down)
+        @pl.when(jnp.logical_and(has_down, jnp.logical_or(not_far, i in (1, 2, 3, 4))))
         def _():
             y_copies[i].start()
 
@@ -337,6 +338,11 @@
         value = jnp.where(group == g, rows[16 * g : 16 * (g + 1)], value)
     pooled_out[:16, :] = value.astype(BF16)
     send_x((POOLED, 6, 7))
+
+    @pl.when(jnp.logical_and(has_down, far))
+    def _():
+        for i in (5, 0):
+            y_copies[i].start()
 
     pl.semaphore_wait(told.at[2], in_group(2))
     tell_group(told.at[3], 4)

time: 22.8 us -> 22.8 us (level)
  no operation moved by 1% of the time
where the time goes in v7:
time: 22.8 us; the launch traced here: 22.6 us
  Pallas kernels  22 us (96%)
  between operations  0.64 us (3%)
    pallas_call x1, Pallas kernels, shards(): pl.pallas_call(kernel, name='blend', out_shape=shapes, in_specs=[hbm] * 5...  20.7 us
    pallas_call x1, Pallas kernels, shards(): pl.pallas_call(store, name='store', out_shape=shapes, in_specs=[pl.BlockS...  1.28 us

profile of v7, /device:TPU:257, one launch (start us, length us, event | category | flops | bytes accessed | tf_op | source)
XLA Modules:
  0.0 22.6 jit_solution(11304972190243684171)
XLA Ops:
  0.6 20.7 %blend.1 = (bf16[6,256,512]{2,1,0:T(8,128)(2,1)S(1)}, bf16[6,128,128]{2,1,0:T(8,128)(2,1)S(1)}, bf16[384,32]{1,0:T(8,128)(2,1)S(1)}, bf16[192,64]{1,0:T(8,128)(2,1)S(1)}, bf16[48,32]{1,0:T(8,128)(2,1)S(1)}) custom-call(bf16[7,256,640]{2,1,0:T(8,128)(2,1)} %bitcast.9, s32[56]{0:T(128)} %weight_x_in.1, s32[40]{0:T(128)} %weight_y_in.1, ...), custom_call_target="tpu_custom_call" | custom-call | tf_op jit(solution)/shard_map/blend/pallas_call | solution.py:542
  21.3 1.3 %store.1 = (bf16[6,256,512]{2,1,0:T(8,128)(2,1)}, bf16[6,128,128]{2,1,0:T(8,128)(2,1)}, bf16[384,32]{1,0:T(8,128)(2,1)}, bf16[192,64]{1,0:T(8,128)(2,1)}, bf16[48,32]{1,0:T(8,128)(2,1)}) custom-call(bf16[6,256,512]{2,1,0:T(8,128)(2,1)S(1)} %get-tuple-element.15.refs_0_, bf16[6,128,128]{2,1,0:T(8,128)(2,1)S(1)} %get-tuple-element.16.refs_1_, ...), custom_call_target="tpu_custom_call" | custom-call | tf_op jit(solution)/shard_map/store/pallas_call | solution.py:602

commit v8 on v7

--- a/solution.py
+++ b/solution.py
@@ -13,7 +13,7 @@
 ROWS = 256
 PIECES = ((1, 0), (1, 1), (2, 0), (2, 1), (3, 0), (3, 1), (0, 0), (0, 1))
 POOLED = 8
-VIA = (2, 1, 1, 1, 0, 0, None, None, None)
+VIA = (1, 1, 0, 0, 2, 1, None, None, None)
 
 
 def iota(shape, dim):

time: 22.8 us -> 22.8 us (level)
  no operation moved by 1% of the time
where the time goes in v8:
time: 22.8 us; the launch traced here: 22.6 us
  Pallas kernels  22 us (96%)
  between operations  0.64 us (3%)
    pallas_call x1, Pallas kernels, shards(): pl.pallas_call(kernel, name='blend', out_shape=shapes, in_specs=[hbm] * 5...  20.7 us
    pallas_call x1, Pallas kernels, shards(): pl.pallas_call(store, name='store', out_shape=shapes, in_specs=[pl.BlockS...  1.28 us

profile of v8, /device:TPU:257, one launch (start us, length us, event | category | flops | bytes accessed | tf_op | source)
XLA Modules:
  0.0 22.6 jit_solution(1727846324850122869)
XLA Ops:
  0.6 20.7 %blend.1 = (bf16[6,256,512]{2,1,0:T(8,128)(2,1)S(1)}, bf16[6,128,128]{2,1,0:T(8,128)(2,1)S(1)}, bf16[384,32]{1,0:T(8,128)(2,1)S(1)}, bf16[192,64]{1,0:T(8,128)(2,1)S(1)}, bf16[48,32]{1,0:T(8,128)(2,1)S(1)}) custom-call(bf16[7,256,640]{2,1,0:T(8,128)(2,1)} %bitcast.9, s32[56]{0:T(128)} %weight_x_in.1, s32[40]{0:T(128)} %weight_y_in.1, ...), custom_call_target="tpu_custom_call" | custom-call | tf_op jit(solution)/shard_map/blend/pallas_call | solution.py:542
  21.3 1.3 %store.1 = (bf16[6,256,512]{2,1,0:T(8,128)(2,1)}, bf16[6,128,128]{2,1,0:T(8,128)(2,1)}, bf16[384,32]{1,0:T(8,128)(2,1)}, bf16[192,64]{1,0:T(8,128)(2,1)}, bf16[48,32]{1,0:T(8,128)(2,1)}) custom-call(bf16[6,256,512]{2,1,0:T(8,128)(2,1)S(1)} %get-tuple-element.15.refs_0_, bf16[6,128,128]{2,1,0:T(8,128)(2,1)S(1)} %get-tuple-element.16.refs_1_, ...), custom_call_target="tpu_custom_call" | custom-call | tf_op jit(solution)/shard_map/store/pallas_call | solution.py:602
